TPU v7x, 128 devices: a whole 4x4x4 slice. The times are simulated.
128 devices in a mesh: blk: 16 (over x, y_lo, core), req: 2 (over y_hi), head: 4 (over z).
Axes of the slice: x: 4, y: 4 (y_hi: 2, y_lo: 2; y = y_hi * 2 + y_lo), z: 4, core: 2. Of those that a mesh axis runs over, the one named last changes fastest.
Arguments:
- query: bfloat16 [8192, 4096], P(('blk', 'req'), 'head'), may hold values from -6 to 6
- key_comp: bfloat16 [8192, 512], P(('blk', 'req'), 'head'), may hold values from -5 to 5
- value_comp: bfloat16 [8192, 512], P(('blk', 'req'), 'head'), may hold values from -5 to 5
- key_prompt: bfloat16 [6144, 512], P('blk', 'head'), may hold values from -6 to 6
- value_prompt: bfloat16 [6144, 512], P('blk', 'head'), may hold values from -5 to 5
- out: bfloat16 [8192, 4096], P(('blk', 'req'), 'head'), may hold values from -5 to 5
- d_out: bfloat16 [8192, 4096], P(('blk', 'req'), 'head'), may hold values from -80 to 80
- steps: int32 [8192], P(('blk', 'req')), may hold values from 0 to 63
Outputs:
- grad_query: bfloat16 [8192, 4096], P(('blk', 'req'), 'head')
- grad_key_comp: bfloat16 [8192, 512], P(('blk', 'req'), 'head')
- grad_value_comp: bfloat16 [8192, 512], P(('blk', 'req'), 'head')
- grad_key_prompt: bfloat16 [6144, 512], P(('blk', 'req'), 'head')
- grad_value_prompt: bfloat16 [6144, 512], P(('blk', 'req'), 'head')
All inputs are finite; a program needn't handle non-finite values.
Results may differ from a plain program's by a relative error of at most 0.012.
Values may be sent and summed in bfloat16 or wider, within the bound.
No kernel may reach another device: no remote copies, remote signals or barrier semaphores. Data moves between devices by JAX's collectives and lax.ppermute only.
A program may use at most 192 MiB of HBM per device.

v0:
```python
import jax
import jax.numpy as jnp
from jax import lax
from jax.sharding import PartitionSpec as P

HD = 128
GROUP = 8


def from_behind(block, axis, distance):
    devices = range(lax.axis_size(axis))
    route = [((i - distance) % len(devices), i) for i in devices]
    return lax.ppermute(block, axis, route)


def attend_back(query_heads, grad_heads, log_total, out_dot, key_rows, value_rows):
    score_scale = HD ** (-0.5)
    row_count = key_rows.shape[0]
    kv_local = query_heads.shape[1]
    key_heads = key_rows.reshape(row_count, kv_local, HD)
    value_heads = value_rows.reshape(row_count, kv_local, HD)
    scores = (
        jnp.einsum("tgnd,pgd->tgnp", query_heads, key_heads, preferred_element_type=jnp.float32)
        * score_scale
    )
    prob_full = jnp.exp(scores - log_total[..., None])
    grad_prob = jnp.einsum(
        "tgnd,pgd->tgnp", grad_heads, value_heads, preferred_element_type=jnp.float32
    )
    grad_score = (prob_full * (grad_prob - out_dot[..., None])).astype(jnp.bfloat16)
    part_query = jnp.einsum(
        "tgnp,pgd->tgnd", grad_score, key_heads, preferred_element_type=jnp.float32
    )
    part_key = jnp.einsum(
        "tgnp,tgnd->pgd", grad_score, query_heads, preferred_element_type=jnp.float32
    )
    part_value = jnp.einsum(
        "tgnp,tgnd->pgd",
        prob_full.astype(jnp.bfloat16),
        grad_heads,
        preferred_element_type=jnp.float32,
    )
    return (part_query, part_key, part_value)


def shards(query, key_comp, value_comp, key_prompt, value_prompt, out, d_out, steps):
    score_scale = HD ** (-0.5)
    tokens = query.shape[0]
    kv_local = key_comp.shape[1] // HD
    shard_rows = key_prompt.shape[0]
    loop_size = lax.axis_size("blk")
    query_heads = query.reshape(tokens, kv_local, GROUP, HD)
    grad_heads = d_out.reshape(tokens, kv_local, GROUP, HD)
    self_keys = key_comp.reshape(tokens, kv_local, HD)
    self_values = value_comp.reshape(tokens, kv_local, HD)
    visible = steps[None, :] <= steps[:, None]
    self_scores = (
        jnp.einsum("tgnd,jgd->tgnj", query_heads, self_keys, preferred_element_type=jnp.float32)
        * score_scale
    )
    self_scores = jnp.where(visible[:, None, None, :], self_scores, -jnp.inf)
    start_max = self_scores.max(-1)
    start_total = jnp.exp(self_scores - start_max[..., None]).sum(-1)
    shard_piece = lax.all_gather(key_prompt, "blk", axis=0, tiled=True)
    piece_keys = shard_piece.reshape(shard_piece.shape[0], kv_local, HD)
    scores = (
        jnp.einsum("tgnd,pgd->tgnp", query_heads, piece_keys, preferred_element_type=jnp.float32)
        * score_scale
    )
    new_max = jnp.maximum(start_max, scores.max(-1))
    new_total = start_total * jnp.exp(start_max - new_max) + jnp.exp(
        scores - new_max[..., None]
    ).sum(-1)
    log_total = new_max + jnp.log(new_total)
    out_dot = (
        (d_out.astype(jnp.float32) * out.astype(jnp.float32))
        .reshape(tokens, kv_local, GROUP, HD)
        .sum(-1)
    )
    self_probs = jnp.exp(self_scores - log_total[..., None])
    self_dprob = jnp.einsum(
        "tgnd,jgd->tgnj", grad_heads, self_values, preferred_element_type=jnp.float32
    )
    self_dscore = (self_probs * (self_dprob - out_dot[..., None])).astype(jnp.bfloat16)
    self_query = jnp.einsum(
        "tgnj,jgd->tgnd", self_dscore, self_keys, preferred_element_type=jnp.float32
    )
    grad_kc = score_scale * jnp.einsum(
        "tgnj,tgnd->jgd", self_dscore, query_heads, preferred_element_type=jnp.float32
    )
    grad_vc = jnp.einsum(
        "tgnj,tgnd->jgd",
        self_probs.astype(jnp.bfloat16),
        grad_heads,
        preferred_element_type=jnp.float32,
    )
    zero_query = jnp.zeros((tokens, kv_local, GROUP, HD), jnp.float32)
    zero_prompt = jnp.zeros((shard_rows, kv_local, HD), jnp.float32)

    def advance(step_index, running):
        moving_keys, moving_values, key_acc, value_acc, query_acc = running
        part_query, part_key, part_value = attend_back(
            query_heads, grad_heads, log_total, out_dot, moving_keys, moving_values
        )
        moving_keys, moving_values = from_behind((moving_keys, moving_values), "blk", 1)
        key_acc, value_acc = from_behind((key_acc + part_key, value_acc + part_value), "blk", 1)
        return (moving_keys, moving_values, key_acc, value_acc, query_acc + part_query)

    final = lax.fori_loop(
        0, loop_size, advance, (key_prompt, value_prompt, zero_prompt, zero_prompt, zero_query)
    )
    key_acc, value_acc, query_acc = (final[2], final[3], final[4])
    key_sum, value_sum = (
        lax.psum_scatter(
            (score_scale * key_acc).reshape(shard_rows, -1).astype(jnp.bfloat16),
            "req",
            scatter_dimension=0,
            tiled=True,
        ).astype(jnp.float32),
        lax.psum_scatter(
            value_acc.reshape(shard_rows, -1).astype(jnp.bfloat16),
            "req",
            scatter_dimension=0,
            tiled=True,
        ).astype(jnp.float32),
    )
    grad_query = (score_scale * (self_query + query_acc)).astype(jnp.bfloat16).reshape(tokens, -1)
    grad_key_comp = grad_kc.astype(jnp.bfloat16).reshape(tokens, -1)
    grad_value_comp = grad_vc.astype(jnp.bfloat16).reshape(tokens, -1)
    return (
        grad_query,
        grad_key_comp,
        grad_value_comp,
        key_sum.astype(jnp.bfloat16),
        value_sum.astype(jnp.bfloat16),
    )


def solution(mesh):
    placed = (
        P(("blk", "req"), "head"),
        P(("blk", "req"), "head"),
        P(("blk", "req"), "head"),
        P("blk", "head"),
        P("blk", "head"),
        P(("blk", "req"), "head"),
        P(("blk", "req"), "head"),
        P(("blk", "req")),
    )
    return jax.shard_map(
        shards,
        mesh=mesh,
        in_specs=placed,
        out_specs=(
            P(("blk", "req"), "head"),
            P(("blk", "req"), "head"),
            P(("blk", "req"), "head"),
            P(("blk", "req"), "head"),
            P(("blk", "req"), "head"),
        ),
        check_vma=False,
    )
```

profile of v0, /device:TPU:1, one launch (start us, length us, event | category | flops | bytes accessed | tf_op | source)
XLA Modules:
  0.0 358.9 jit_solution(6492766142528703328)
XLA Ops:
  7.2 1.5 copy.105
  8.8 1.5 copy.106
  11.6 1.4 multiply_bitcast_fusion
  15.4 1.3 copy-done.1
  17.1 30.1 %all-gather.2.cloned.1.call-done = bf16[6144,128]{1,0:T(8,128)(2,1)} async-done(((bf16[384,128]{1,0:T(8,128)(2,1)}), bf16[6144,128]{1,0:T(8,128)(2,1)}) %all-gather.2.cloned.1.call-update) | async-done | bytes 1572880 | tf_op jit(solution)/shard_map/all_gather | solution.py:64
  47.2 20.7 %bitcast_reduce_fusion = (f32[256,8]{0,1:T(8,128)S(1)}, f32[6144,256,8]{1,0,2:T(8,128)}) fusion(bf16[6144,128]{1,0:T(8,128)(2,1)} %all-gather.2.cloned.1.call-done, bf16[256,1024]{1,0:T(8,128)(2,1)S(1)} %copy-done.4), kind=kOutput, calls=%fused_computation.30 | convolution fusion | flops 3246389248 | bytes 52436992 | tf_op jit(solution)/shard_map/tgnd,pgd->tgnp/dot_general | solution.py:67
  67.9 20.1 %fusion.41 = f32[256,8]{0,1:T(8,128)S(1)} fusion(f32[6144,256,8]{1,0,2:T(8,128)} %get-tuple-element.153, f32[256,8]{0,1:T(8,128)S(1)} %max.21), kind=kLoop, calls=%fused_computation.32 | loop fusion | flops 37746688 | bytes 50348032 | tf_op jit(solution)/shard_map/reduce_sum | solution.py:73
  88.0 221.6 %while.19 = (s32[]{:T(128)}, bf16[384,128]{1,0:T(8,128)(2,1)}, bf16[384,128]{1,0:T(8,128)(2,1)}, f32[384,1,128]{2,0,1:T(8,128)S(1)}, f32[384,1,128]{2,0,1:T(8,12...) while((s32[]{:T(128)}, bf16[384,128]{1,0:T(8,128)(2,1)}, ...), condition=%wide.region_6.7_spmd.clone, body=%wide.region_5.6_spmd.clone.sunk | while | flops 1013547008 | bytes 22208796 | solution.py:109
  93.8 1.3 collective-permute-start.2
  96.1 1.6 fusion.110
  98.0 2.0 collective-permute-done.3
  100.9 2.5 collective-permute-start
  107.0 1.8 collective-permute-start.2
  109.6 2.8 fusion.110
  112.4 1.3 collective-permute-done.3
  114.7 2.5 collective-permute-start
  120.7 1.6 collective-permute-start.2
  123.1 2.8 fusion.110
  128.1 2.5 collective-permute-start
  134.2 2.2 collective-permute-start.2
  137.1 2.8 fusion.110
  142.2 2.5 collective-permute-start
  148.2 1.6 collective-permute-start.2
  150.6 2.8 fusion.110
  155.6 2.5 collective-permute-start
  161.7 1.8 collective-permute-start.2
  164.3 2.8 fusion.110
  169.3 2.5 collective-permute-start
  175.4 2.2 collective-permute-start.2
  178.4 2.8 fusion.110
  183.4 2.5 collective-permute-start
  189.5 3.4 collective-permute-start.2
  193.6 2.8 fusion.110
  198.7 2.5 collective-permute-start
  204.7 2.1 collective-permute-start.2
  207.6 2.8 fusion.110
  212.7 2.5 collective-permute-start
  218.7 2.1 collective-permute-start.2
  221.6 2.8 fusion.110
  226.6 2.5 collective-permute-start
  232.7 2.1 collective-permute-start.2
  235.6 2.8 fusion.110
  240.6 2.5 collective-permute-start
  246.7 2.1 collective-permute-start.2
  249.5 2.8 fusion.110
  254.6 2.5 collective-permute-start
  260.6 2.1 collective-permute-start.2
  263.5 2.8 fusion.110
  268.6 2.5 collective-permute-start
  274.6 2.1 collective-permute-start.2
  277.5 2.8 fusion.110
  282.5 2.5 collective-permute-start
  288.6 2.1 collective-permute-start.2
  291.5 2.8 fusion.110
  296.5 2.5 collective-permute-start
  302.6 2.1 collective-permute-start.2
  305.5 2.8 fusion.110
  309.6 2.7 copy.49
  312.3 2.1 fusion.51
  314.5 1.5 fusion.46
  316.0 1.7 fusion.49
  320.1 2.3 fusion.52
  322.3 13.6 %reduce-scatter.3.cloned.1.call-done = bf16[192,128]{1,0:T(8,128)(2,1)} async-done(((bf16[384,128]{1,0:T(8,128)(2,1)}), bf16[192,128]{1,0:T(8,128)(2,1)}) %reduce-scatter.3.cloned.1.call-update) | async-done | bytes 49168 | tf_op jit(solution)/shard_map/reduce_scatter | solution.py:114
  336.0 16.4 %reduce-scatter.5.cloned.1.call-done = bf16[192,128]{1,0:T(8,128)(2,1)} async-done(((bf16[384,128]{1,0:T(8,128)(2,1)}), bf16[192,128]{1,0:T(8,128)(2,1)}) %reduce-scatter.5.cloned.1.call-update) | async-done | bytes 49168 | tf_op jit(solution)/shard_map/reduce_scatter | solution.py:120
  (234 shorter events, 109.9 us)
Async XLA Ops:
  7.2 40.0 %all-gather.2.cloned.1.call-start = ((), (), s32[]{:S(2)}) async-start(), calls=%async_computation.2 | async-start | bytes 1671168 | tf_op jit(solution)/shard_map/all_gather | solution.py:64
  10.3 325.7 %reduce-scatter.3.cloned.1.call-start = ((), (), s32[]{:S(2)}) async-start(), calls=%async_computation.3 | async-start | bytes 147456 | tf_op jit(solution)/shard_map/reduce_scatter | solution.py:114
  88.9 8.8 %collective-permute-start = (bf16[384,128]{1,0:T(8,128)(2,1)S(1)}, bf16[384,128]{1,0:T(8,128)(2,1)}, u32[]{:S(2)}, u32[]{:S(2)}) collective-permute-start(bf16[384,128]{1,0:T(8,128)(2,1)S(1)} %copy.91), channel_id=1, source_target_pairs={{120,0},{0,8},{8,16},{16,24},{24,32},{32,40},{40,48},{48,56},{56,6... | collective-permute-start | bytes 294920 | tf_op jit(solution)/shard_map/while/body/eval_jaxpr/ppermute | solution.py:13
  90.9 6.8 %collective-permute-start.1 = (bf16[384,128]{1,0:T(8,128)(2,1)S(1)}, bf16[384,128]{1,0:T(8,128)(2,1)}, u32[]{:S(2)}, u32[]{:S(2)}) collective-permute-start(bf16[384,128]{1,0:T(8,128)(2,1)S(1)} %copy.92), channel_id=1, source_target_pairs={{120,0},{0,8},{8,16},{16,24},{24,32},{32,40},{40,48},{48,56},{56,6... | collective-permute-start | bytes 294920 | tf_op jit(solution)/shard_map/while/body/eval_jaxpr/ppermute | solution.py:13
  95.8 4.3 %collective-permute-start.3 = (f32[384,1,128]{2,0,1:T(8,128)S(1)}, f32[384,1,128]{2,0,1:T(8,128)S(1)}, u32[]{:S(2)}, u32[]{:S(2)}) collective-permute-start(f32[384,1,128]{2,0,1:T(8,128)S(1)} %fusion.109), channel_id=1, source_target_pairs={{120,0},{0,8},{8,16},{16,24},{24,32},{32,40},{40,48},{48,56},{56,6... | collective-permute-start | bytes 589832 | tf_op jit(solution)/shard_map/while/body/eval_jaxpr/ppermute | solution.py:13
  100.9 11.5 %collective-permute-start = (bf16[384,128]{1,0:T(8,128)(2,1)S(1)}, bf16[384,128]{1,0:T(8,128)(2,1)}, u32[]{:S(2)}, u32[]{:S(2)}) collective-permute-start(bf16[384,128]{1,0:T(8,128)(2,1)S(1)} %copy.91), channel_id=1, source_target_pairs={{120,0},{0,8},{8,16},{16,24},{24,32},{32,40},{40,48},{48,56},{56,6... | collective-permute-start | bytes 294920 | tf_op jit(solution)/shard_map/while/body/eval_jaxpr/ppermute | solution.py:13
  104.3 8.1 %collective-permute-start.1 = (bf16[384,128]{1,0:T(8,128)(2,1)S(1)}, bf16[384,128]{1,0:T(8,128)(2,1)}, u32[]{:S(2)}, u32[]{:S(2)}) collective-permute-start(bf16[384,128]{1,0:T(8,128)(2,1)S(1)} %copy.92), channel_id=1, source_target_pairs={{120,0},{0,8},{8,16},{16,24},{24,32},{32,40},{40,48},{48,56},{56,6... | collective-permute-start | bytes 294920 | tf_op jit(solution)/shard_map/while/body/eval_jaxpr/ppermute | solution.py:13
  107.0 5.5 %collective-permute-start.2 = (f32[384,1,128]{2,0,1:T(8,128)}, f32[384,1,128]{2,0,1:T(8,128)S(1)}, u32[]{:S(2)}, u32[]{:S(2)}) collective-permute-start(f32[384,1,128]{2,0,1:T(8,128)} %fusion.108), channel_id=1, source_target_pairs={{120,0},{0,8},{8,16},{16,24},{24,32},{32,40},{40,48},{48,56},{56,6... | collective-permute-start | bytes 589832 | tf_op jit(solution)/shard_map/while/body/eval_jaxpr/ppermute | solution.py:13
  109.5 4.3 %collective-permute-start.3 = (f32[384,1,128]{2,0,1:T(8,128)S(1)}, f32[384,1,128]{2,0,1:T(8,128)S(1)}, u32[]{:S(2)}, u32[]{:S(2)}) collective-permute-start(f32[384,1,128]{2,0,1:T(8,128)S(1)} %fusion.109), channel_id=1, source_target_pairs={{120,0},{0,8},{8,16},{16,24},{24,32},{32,40},{40,48},{48,56},{56,6... | collective-permute-start | bytes 589832 | tf_op jit(solution)/shard_map/while/body/eval_jaxpr/ppermute | solution.py:13
  114.7 11.2 %collective-permute-start = (bf16[384,128]{1,0:T(8,128)(2,1)S(1)}, bf16[384,128]{1,0:T(8,128)(2,1)}, u32[]{:S(2)}, u32[]{:S(2)}) collective-permute-start(bf16[384,128]{1,0:T(8,128)(2,1)S(1)} %copy.91), channel_id=1, source_target_pairs={{120,0},{0,8},{8,16},{16,24},{24,32},{32,40},{40,48},{48,56},{56,6... | collective-permute-start | bytes 294920 | tf_op jit(solution)/shard_map/while/body/eval_jaxpr/ppermute | solution.py:13
  118.0 7.9 %collective-permute-start.1 = (bf16[384,128]{1,0:T(8,128)(2,1)S(1)}, bf16[384,128]{1,0:T(8,128)(2,1)}, u32[]{:S(2)}, u32[]{:S(2)}) collective-permute-start(bf16[384,128]{1,0:T(8,128)(2,1)S(1)} %copy.92), channel_id=1, source_target_pairs={{120,0},{0,8},{8,16},{16,24},{24,32},{32,40},{40,48},{48,56},{56,6... | collective-permute-start | bytes 294920 | tf_op jit(solution)/shard_map/while/body/eval_jaxpr/ppermute | solution.py:13
  120.7 5.2 %collective-permute-start.2 = (f32[384,1,128]{2,0,1:T(8,128)}, f32[384,1,128]{2,0,1:T(8,128)S(1)}, u32[]{:S(2)}, u32[]{:S(2)}) collective-permute-start(f32[384,1,128]{2,0,1:T(8,128)} %fusion.108), channel_id=1, source_target_pairs={{120,0},{0,8},{8,16},{16,24},{24,32},{32,40},{40,48},{48,56},{56,6... | collective-permute-start | bytes 589832 | tf_op jit(solution)/shard_map/while/body/eval_jaxpr/ppermute | solution.py:13
  123.0 4.3 %collective-permute-start.3 = (f32[384,1,128]{2,0,1:T(8,128)S(1)}, f32[384,1,128]{2,0,1:T(8,128)S(1)}, u32[]{:S(2)}, u32[]{:S(2)}) collective-permute-start(f32[384,1,128]{2,0,1:T(8,128)S(1)} %fusion.109), channel_id=1, source_target_pairs={{120,0},{0,8},{8,16},{16,24},{24,32},{32,40},{40,48},{48,56},{56,6... | collective-permute-start | bytes 589832 | tf_op jit(solution)/shard_map/while/body/eval_jaxpr/ppermute | solution.py:13
  128.1 11.9 %collective-permute-start = (bf16[384,128]{1,0:T(8,128)(2,1)S(1)}, bf16[384,128]{1,0:T(8,128)(2,1)}, u32[]{:S(2)}, u32[]{:S(2)}) collective-permute-start(bf16[384,128]{1,0:T(8,128)(2,1)S(1)} %copy.91), channel_id=1, source_target_pairs={{120,0},{0,8},{8,16},{16,24},{24,32},{32,40},{40,48},{48,56},{56,6... | collective-permute-start | bytes 294920 | tf_op jit(solution)/shard_map/while/body/eval_jaxpr/ppermute | solution.py:13
  131.5 8.5 %collective-permute-start.1 = (bf16[384,128]{1,0:T(8,128)(2,1)S(1)}, bf16[384,128]{1,0:T(8,128)(2,1)}, u32[]{:S(2)}, u32[]{:S(2)}) collective-permute-start(bf16[384,128]{1,0:T(8,128)(2,1)S(1)} %copy.92), channel_id=1, source_target_pairs={{120,0},{0,8},{8,16},{16,24},{24,32},{32,40},{40,48},{48,56},{56,6... | collective-permute-start | bytes 294920 | tf_op jit(solution)/shard_map/while/body/eval_jaxpr/ppermute | solution.py:13
  134.2 5.8 %collective-permute-start.2 = (f32[384,1,128]{2,0,1:T(8,128)}, f32[384,1,128]{2,0,1:T(8,128)S(1)}, u32[]{:S(2)}, u32[]{:S(2)}) collective-permute-start(f32[384,1,128]{2,0,1:T(8,128)} %fusion.108), channel_id=1, source_target_pairs={{120,0},{0,8},{8,16},{16,24},{24,32},{32,40},{40,48},{48,56},{56,6... | collective-permute-start | bytes 589832 | tf_op jit(solution)/shard_map/while/body/eval_jaxpr/ppermute | solution.py:13
  137.0 4.3 %collective-permute-start.3 = (f32[384,1,128]{2,0,1:T(8,128)S(1)}, f32[384,1,128]{2,0,1:T(8,128)S(1)}, u32[]{:S(2)}, u32[]{:S(2)}) collective-permute-start(f32[384,1,128]{2,0,1:T(8,128)S(1)} %fusion.109), channel_id=1, source_target_pairs={{120,0},{0,8},{8,16},{16,24},{24,32},{32,40},{40,48},{48,56},{56,6... | collective-permute-start | bytes 589832 | tf_op jit(solution)/shard_map/while/body/eval_jaxpr/ppermute | solution.py:13
  142.2 11.2 %collective-permute-start = (bf16[384,128]{1,0:T(8,128)(2,1)S(1)}, bf16[384,128]{1,0:T(8,128)(2,1)}, u32[]{:S(2)}, u32[]{:S(2)}) collective-permute-start(bf16[384,128]{1,0:T(8,128)(2,1)S(1)} %copy.91), channel_id=1, source_target_pairs={{120,0},{0,8},{8,16},{16,24},{24,32},{32,40},{40,48},{48,56},{56,6... | collective-permute-start | bytes 294920 | tf_op jit(solution)/shard_map/while/body/eval_jaxpr/ppermute | solution.py:13
  145.6 7.9 %collective-permute-start.1 = (bf16[384,128]{1,0:T(8,128)(2,1)S(1)}, bf16[384,128]{1,0:T(8,128)(2,1)}, u32[]{:S(2)}, u32[]{:S(2)}) collective-permute-start(bf16[384,128]{1,0:T(8,128)(2,1)S(1)} %copy.92), channel_id=1, source_target_pairs={{120,0},{0,8},{8,16},{16,24},{24,32},{32,40},{40,48},{48,56},{56,6... | collective-permute-start | bytes 294920 | tf_op jit(solution)/shard_map/while/body/eval_jaxpr/ppermute | solution.py:13
  148.2 5.2 %collective-permute-start.2 = (f32[384,1,128]{2,0,1:T(8,128)}, f32[384,1,128]{2,0,1:T(8,128)S(1)}, u32[]{:S(2)}, u32[]{:S(2)}) collective-permute-start(f32[384,1,128]{2,0,1:T(8,128)} %fusion.108), channel_id=1, source_target_pairs={{120,0},{0,8},{8,16},{16,24},{24,32},{32,40},{40,48},{48,56},{56,6... | collective-permute-start | bytes 589832 | tf_op jit(solution)/shard_map/while/body/eval_jaxpr/ppermute | solution.py:13
  150.5 4.3 %collective-permute-start.3 = (f32[384,1,128]{2,0,1:T(8,128)S(1)}, f32[384,1,128]{2,0,1:T(8,128)S(1)}, u32[]{:S(2)}, u32[]{:S(2)}) collective-permute-start(f32[384,1,128]{2,0,1:T(8,128)S(1)} %fusion.109), channel_id=1, source_target_pairs={{120,0},{0,8},{8,16},{16,24},{24,32},{32,40},{40,48},{48,56},{56,6... | collective-permute-start | bytes 589832 | tf_op jit(solution)/shard_map/while/body/eval_jaxpr/ppermute | solution.py:13
  155.6 11.5 %collective-permute-start = (bf16[384,128]{1,0:T(8,128)(2,1)S(1)}, bf16[384,128]{1,0:T(8,128)(2,1)}, u32[]{:S(2)}, u32[]{:S(2)}) collective-permute-start(bf16[384,128]{1,0:T(8,128)(2,1)S(1)} %copy.91), channel_id=1, source_target_pairs={{120,0},{0,8},{8,16},{16,24},{24,32},{32,40},{40,48},{48,56},{56,6... | collective-permute-start | bytes 294920 | tf_op jit(solution)/shard_map/while/body/eval_jaxpr/ppermute | solution.py:13
  159.0 8.1 %collective-permute-start.1 = (bf16[384,128]{1,0:T(8,128)(2,1)S(1)}, bf16[384,128]{1,0:T(8,128)(2,1)}, u32[]{:S(2)}, u32[]{:S(2)}) collective-permute-start(bf16[384,128]{1,0:T(8,128)(2,1)S(1)} %copy.92), channel_id=1, source_target_pairs={{120,0},{0,8},{8,16},{16,24},{24,32},{32,40},{40,48},{48,56},{56,6... | collective-permute-start | bytes 294920 | tf_op jit(solution)/shard_map/while/body/eval_jaxpr/ppermute | solution.py:13
  161.7 5.4 %collective-permute-start.2 = (f32[384,1,128]{2,0,1:T(8,128)}, f32[384,1,128]{2,0,1:T(8,128)S(1)}, u32[]{:S(2)}, u32[]{:S(2)}) collective-permute-start(f32[384,1,128]{2,0,1:T(8,128)} %fusion.108), channel_id=1, source_target_pairs={{120,0},{0,8},{8,16},{16,24},{24,32},{32,40},{40,48},{48,56},{56,6... | collective-permute-start | bytes 589832 | tf_op jit(solution)/shard_map/while/body/eval_jaxpr/ppermute | solution.py:13
  164.2 4.3 %collective-permute-start.3 = (f32[384,1,128]{2,0,1:T(8,128)S(1)}, f32[384,1,128]{2,0,1:T(8,128)S(1)}, u32[]{:S(2)}, u32[]{:S(2)}) collective-permute-start(f32[384,1,128]{2,0,1:T(8,128)S(1)} %fusion.109), channel_id=1, source_target_pairs={{120,0},{0,8},{8,16},{16,24},{24,32},{32,40},{40,48},{48,56},{56,6... | collective-permute-start | bytes 589832 | tf_op jit(solution)/shard_map/while/body/eval_jaxpr/ppermute | solution.py:13
  169.3 11.9 %collective-permute-start = (bf16[384,128]{1,0:T(8,128)(2,1)S(1)}, bf16[384,128]{1,0:T(8,128)(2,1)}, u32[]{:S(2)}, u32[]{:S(2)}) collective-permute-start(bf16[384,128]{1,0:T(8,128)(2,1)S(1)} %copy.91), channel_id=1, source_target_pairs={{120,0},{0,8},{8,16},{16,24},{24,32},{32,40},{40,48},{48,56},{56,6... | collective-permute-start | bytes 294920 | tf_op jit(solution)/shard_map/while/body/eval_jaxpr/ppermute | solution.py:13
  172.7 8.5 %collective-permute-start.1 = (bf16[384,128]{1,0:T(8,128)(2,1)S(1)}, bf16[384,128]{1,0:T(8,128)(2,1)}, u32[]{:S(2)}, u32[]{:S(2)}) collective-permute-start(bf16[384,128]{1,0:T(8,128)(2,1)S(1)} %copy.92), channel_id=1, source_target_pairs={{120,0},{0,8},{8,16},{16,24},{24,32},{32,40},{40,48},{48,56},{56,6... | collective-permute-start | bytes 294920 | tf_op jit(solution)/shard_map/while/body/eval_jaxpr/ppermute | solution.py:13
  175.4 5.8 %collective-permute-start.2 = (f32[384,1,128]{2,0,1:T(8,128)}, f32[384,1,128]{2,0,1:T(8,128)S(1)}, u32[]{:S(2)}, u32[]{:S(2)}) collective-permute-start(f32[384,1,128]{2,0,1:T(8,128)} %fusion.108), channel_id=1, source_target_pairs={{120,0},{0,8},{8,16},{16,24},{24,32},{32,40},{40,48},{48,56},{56,6... | collective-permute-start | bytes 589832 | tf_op jit(solution)/shard_map/while/body/eval_jaxpr/ppermute | solution.py:13
  178.2 4.3 %collective-permute-start.3 = (f32[384,1,128]{2,0,1:T(8,128)S(1)}, f32[384,1,128]{2,0,1:T(8,128)S(1)}, u32[]{:S(2)}, u32[]{:S(2)}) collective-permute-start(f32[384,1,128]{2,0,1:T(8,128)S(1)} %fusion.109), channel_id=1, source_target_pairs={{120,0},{0,8},{8,16},{16,24},{24,32},{32,40},{40,48},{48,56},{56,6... | collective-permute-start | bytes 589832 | tf_op jit(solution)/shard_map/while/body/eval_jaxpr/ppermute | solution.py:13
  183.4 13.1 %collective-permute-start = (bf16[384,128]{1,0:T(8,128)(2,1)S(1)}, bf16[384,128]{1,0:T(8,128)(2,1)}, u32[]{:S(2)}, u32[]{:S(2)}) collective-permute-start(bf16[384,128]{1,0:T(8,128)(2,1)S(1)} %copy.91), channel_id=1, source_target_pairs={{120,0},{0,8},{8,16},{16,24},{24,32},{32,40},{40,48},{48,56},{56,6... | collective-permute-start | bytes 294920 | tf_op jit(solution)/shard_map/while/body/eval_jaxpr/ppermute | solution.py:13
  186.8 9.7 %collective-permute-start.1 = (bf16[384,128]{1,0:T(8,128)(2,1)S(1)}, bf16[384,128]{1,0:T(8,128)(2,1)}, u32[]{:S(2)}, u32[]{:S(2)}) collective-permute-start(bf16[384,128]{1,0:T(8,128)(2,1)S(1)} %copy.92), channel_id=1, source_target_pairs={{120,0},{0,8},{8,16},{16,24},{24,32},{32,40},{40,48},{48,56},{56,6... | collective-permute-start | bytes 294920 | tf_op jit(solution)/shard_map/while/body/eval_jaxpr/ppermute | solution.py:13
  189.5 7.0 %collective-permute-start.2 = (f32[384,1,128]{2,0,1:T(8,128)}, f32[384,1,128]{2,0,1:T(8,128)S(1)}, u32[]{:S(2)}, u32[]{:S(2)}) collective-permute-start(f32[384,1,128]{2,0,1:T(8,128)} %fusion.108), channel_id=1, source_target_pairs={{120,0},{0,8},{8,16},{16,24},{24,32},{32,40},{40,48},{48,56},{56,6... | collective-permute-start | bytes 589832 | tf_op jit(solution)/shard_map/while/body/eval_jaxpr/ppermute | solution.py:13
  193.5 4.3 %collective-permute-start.3 = (f32[384,1,128]{2,0,1:T(8,128)S(1)}, f32[384,1,128]{2,0,1:T(8,128)S(1)}, u32[]{:S(2)}, u32[]{:S(2)}) collective-permute-start(f32[384,1,128]{2,0,1:T(8,128)S(1)} %fusion.109), channel_id=1, source_target_pairs={{120,0},{0,8},{8,16},{16,24},{24,32},{32,40},{40,48},{48,56},{56,6... | collective-permute-start | bytes 589832 | tf_op jit(solution)/shard_map/while/body/eval_jaxpr/ppermute | solution.py:13
  198.7 11.8 %collective-permute-start = (bf16[384,128]{1,0:T(8,128)(2,1)S(1)}, bf16[384,128]{1,0:T(8,128)(2,1)}, u32[]{:S(2)}, u32[]{:S(2)}) collective-permute-start(bf16[384,128]{1,0:T(8,128)(2,1)S(1)} %copy.91), channel_id=1, source_target_pairs={{120,0},{0,8},{8,16},{16,24},{24,32},{32,40},{40,48},{48,56},{56,6... | collective-permute-start | bytes 294920 | tf_op jit(solution)/shard_map/while/body/eval_jaxpr/ppermute | solution.py:13
  202.1 8.4 %collective-permute-start.1 = (bf16[384,128]{1,0:T(8,128)(2,1)S(1)}, bf16[384,128]{1,0:T(8,128)(2,1)}, u32[]{:S(2)}, u32[]{:S(2)}) collective-permute-start(bf16[384,128]{1,0:T(8,128)(2,1)S(1)} %copy.92), channel_id=1, source_target_pairs={{120,0},{0,8},{8,16},{16,24},{24,32},{32,40},{40,48},{48,56},{56,6... | collective-permute-start | bytes 294920 | tf_op jit(solution)/shard_map/while/body/eval_jaxpr/ppermute | solution.py:13
  204.7 5.7 %collective-permute-start.2 = (f32[384,1,128]{2,0,1:T(8,128)}, f32[384,1,128]{2,0,1:T(8,128)S(1)}, u32[]{:S(2)}, u32[]{:S(2)}) collective-permute-start(f32[384,1,128]{2,0,1:T(8,128)} %fusion.108), channel_id=1, source_target_pairs={{120,0},{0,8},{8,16},{16,24},{24,32},{32,40},{40,48},{48,56},{56,6... | collective-permute-start | bytes 589832 | tf_op jit(solution)/shard_map/while/body/eval_jaxpr/ppermute | solution.py:13
  207.5 4.3 %collective-permute-start.3 = (f32[384,1,128]{2,0,1:T(8,128)S(1)}, f32[384,1,128]{2,0,1:T(8,128)S(1)}, u32[]{:S(2)}, u32[]{:S(2)}) collective-permute-start(f32[384,1,128]{2,0,1:T(8,128)S(1)} %fusion.109), channel_id=1, source_target_pairs={{120,0},{0,8},{8,16},{16,24},{24,32},{32,40},{40,48},{48,56},{56,6... | collective-permute-start | bytes 589832 | tf_op jit(solution)/shard_map/while/body/eval_jaxpr/ppermute | solution.py:13
  212.7 11.8 %collective-permute-start = (bf16[384,128]{1,0:T(8,128)(2,1)S(1)}, bf16[384,128]{1,0:T(8,128)(2,1)}, u32[]{:S(2)}, u32[]{:S(2)}) collective-permute-start(bf16[384,128]{1,0:T(8,128)(2,1)S(1)} %copy.91), channel_id=1, source_target_pairs={{120,0},{0,8},{8,16},{16,24},{24,32},{32,40},{40,48},{48,56},{56,6... | collective-permute-start | bytes 294920 | tf_op jit(solution)/shard_map/while/body/eval_jaxpr/ppermute | solution.py:13
  216.0 8.4 %collective-permute-start.1 = (bf16[384,128]{1,0:T(8,128)(2,1)S(1)}, bf16[384,128]{1,0:T(8,128)(2,1)}, u32[]{:S(2)}, u32[]{:S(2)}) collective-permute-start(bf16[384,128]{1,0:T(8,128)(2,1)S(1)} %copy.92), channel_id=1, source_target_pairs={{120,0},{0,8},{8,16},{16,24},{24,32},{32,40},{40,48},{48,56},{56,6... | collective-permute-start | bytes 294920 | tf_op jit(solution)/shard_map/while/body/eval_jaxpr/ppermute | solution.py:13
  218.7 5.7 %collective-permute-start.2 = (f32[384,1,128]{2,0,1:T(8,128)}, f32[384,1,128]{2,0,1:T(8,128)S(1)}, u32[]{:S(2)}, u32[]{:S(2)}) collective-permute-start(f32[384,1,128]{2,0,1:T(8,128)} %fusion.108), channel_id=1, source_target_pairs={{120,0},{0,8},{8,16},{16,24},{24,32},{32,40},{40,48},{48,56},{56,6... | collective-permute-start | bytes 589832 | tf_op jit(solution)/shard_map/while/body/eval_jaxpr/ppermute | solution.py:13
  221.5 4.3 %collective-permute-start.3 = (f32[384,1,128]{2,0,1:T(8,128)S(1)}, f32[384,1,128]{2,0,1:T(8,128)S(1)}, u32[]{:S(2)}, u32[]{:S(2)}) collective-permute-start(f32[384,1,128]{2,0,1:T(8,128)S(1)} %fusion.109), channel_id=1, source_target_pairs={{120,0},{0,8},{8,16},{16,24},{24,32},{32,40},{40,48},{48,56},{56,6... | collective-permute-start | bytes 589832 | tf_op jit(solution)/shard_map/while/body/eval_jaxpr/ppermute | solution.py:13
  226.6 11.8 %collective-permute-start = (bf16[384,128]{1,0:T(8,128)(2,1)S(1)}, bf16[384,128]{1,0:T(8,128)(2,1)}, u32[]{:S(2)}, u32[]{:S(2)}) collective-permute-start(bf16[384,128]{1,0:T(8,128)(2,1)S(1)} %copy.91), channel_id=1, source_target_pairs={{120,0},{0,8},{8,16},{16,24},{24,32},{32,40},{40,48},{48,56},{56,6... | collective-permute-start | bytes 294920 | tf_op jit(solution)/shard_map/while/body/eval_jaxpr/ppermute | solution.py:13
  230.0 8.4 %collective-permute-start.1 = (bf16[384,128]{1,0:T(8,128)(2,1)S(1)}, bf16[384,128]{1,0:T(8,128)(2,1)}, u32[]{:S(2)}, u32[]{:S(2)}) collective-permute-start(bf16[384,128]{1,0:T(8,128)(2,1)S(1)} %copy.92), channel_id=1, source_target_pairs={{120,0},{0,8},{8,16},{16,24},{24,32},{32,40},{40,48},{48,56},{56,6... | collective-permute-start | bytes 294920 | tf_op jit(solution)/shard_map/while/body/eval_jaxpr/ppermute | solution.py:13
  232.7 5.7 %collective-permute-start.2 = (f32[384,1,128]{2,0,1:T(8,128)}, f32[384,1,128]{2,0,1:T(8,128)S(1)}, u32[]{:S(2)}, u32[]{:S(2)}) collective-permute-start(f32[384,1,128]{2,0,1:T(8,128)} %fusion.108), channel_id=1, source_target_pairs={{120,0},{0,8},{8,16},{16,24},{24,32},{32,40},{40,48},{48,56},{56,6... | collective-permute-start | bytes 589832 | tf_op jit(solution)/shard_map/while/body/eval_jaxpr/ppermute | solution.py:13
  235.5 4.3 %collective-permute-start.3 = (f32[384,1,128]{2,0,1:T(8,128)S(1)}, f32[384,1,128]{2,0,1:T(8,128)S(1)}, u32[]{:S(2)}, u32[]{:S(2)}) collective-permute-start(f32[384,1,128]{2,0,1:T(8,128)S(1)} %fusion.109), channel_id=1, source_target_pairs={{120,0},{0,8},{8,16},{16,24},{24,32},{32,40},{40,48},{48,56},{56,6... | collective-permute-start | bytes 589832 | tf_op jit(solution)/shard_map/while/body/eval_jaxpr/ppermute | solution.py:13
  240.6 11.8 %collective-permute-start = (bf16[384,128]{1,0:T(8,128)(2,1)S(1)}, bf16[384,128]{1,0:T(8,128)(2,1)}, u32[]{:S(2)}, u32[]{:S(2)}) collective-permute-start(bf16[384,128]{1,0:T(8,128)(2,1)S(1)} %copy.91), channel_id=1, source_target_pairs={{120,0},{0,8},{8,16},{16,24},{24,32},{32,40},{40,48},{48,56},{56,6... | collective-permute-start | bytes 294920 | tf_op jit(solution)/shard_map/while/body/eval_jaxpr/ppermute | solution.py:13
  244.0 8.4 %collective-permute-start.1 = (bf16[384,128]{1,0:T(8,128)(2,1)S(1)}, bf16[384,128]{1,0:T(8,128)(2,1)}, u32[]{:S(2)}, u32[]{:S(2)}) collective-permute-start(bf16[384,128]{1,0:T(8,128)(2,1)S(1)} %copy.92), channel_id=1, source_target_pairs={{120,0},{0,8},{8,16},{16,24},{24,32},{32,40},{40,48},{48,56},{56,6... | collective-permute-start | bytes 294920 | tf_op jit(solution)/shard_map/while/body/eval_jaxpr/ppermute | solution.py:13
  246.7 5.7 %collective-permute-start.2 = (f32[384,1,128]{2,0,1:T(8,128)}, f32[384,1,128]{2,0,1:T(8,128)S(1)}, u32[]{:S(2)}, u32[]{:S(2)}) collective-permute-start(f32[384,1,128]{2,0,1:T(8,128)} %fusion.108), channel_id=1, source_target_pairs={{120,0},{0,8},{8,16},{16,24},{24,32},{32,40},{40,48},{48,56},{56,6... | collective-permute-start | bytes 589832 | tf_op jit(solution)/shard_map/while/body/eval_jaxpr/ppermute | solution.py:13
  249.5 4.3 %collective-permute-start.3 = (f32[384,1,128]{2,0,1:T(8,128)S(1)}, f32[384,1,128]{2,0,1:T(8,128)S(1)}, u32[]{:S(2)}, u32[]{:S(2)}) collective-permute-start(f32[384,1,128]{2,0,1:T(8,128)S(1)} %fusion.109), channel_id=1, source_target_pairs={{120,0},{0,8},{8,16},{16,24},{24,32},{32,40},{40,48},{48,56},{56,6... | collective-permute-start | bytes 589832 | tf_op jit(solution)/shard_map/while/body/eval_jaxpr/ppermute | solution.py:13
  254.6 11.8 %collective-permute-start = (bf16[384,128]{1,0:T(8,128)(2,1)S(1)}, bf16[384,128]{1,0:T(8,128)(2,1)}, u32[]{:S(2)}, u32[]{:S(2)}) collective-permute-start(bf16[384,128]{1,0:T(8,128)(2,1)S(1)} %copy.91), channel_id=1, source_target_pairs={{120,0},{0,8},{8,16},{16,24},{24,32},{32,40},{40,48},{48,56},{56,6... | collective-permute-start | bytes 294920 | tf_op jit(solution)/shard_map/while/body/eval_jaxpr/ppermute | solution.py:13
  258.0 8.4 %collective-permute-start.1 = (bf16[384,128]{1,0:T(8,128)(2,1)S(1)}, bf16[384,128]{1,0:T(8,128)(2,1)}, u32[]{:S(2)}, u32[]{:S(2)}) collective-permute-start(bf16[384,128]{1,0:T(8,128)(2,1)S(1)} %copy.92), channel_id=1, source_target_pairs={{120,0},{0,8},{8,16},{16,24},{24,32},{32,40},{40,48},{48,56},{56,6... | collective-permute-start | bytes 294920 | tf_op jit(solution)/shard_map/while/body/eval_jaxpr/ppermute | solution.py:13
  260.6 5.7 %collective-permute-start.2 = (f32[384,1,128]{2,0,1:T(8,128)}, f32[384,1,128]{2,0,1:T(8,128)S(1)}, u32[]{:S(2)}, u32[]{:S(2)}) collective-permute-start(f32[384,1,128]{2,0,1:T(8,128)} %fusion.108), channel_id=1, source_target_pairs={{120,0},{0,8},{8,16},{16,24},{24,32},{32,40},{40,48},{48,56},{56,6... | collective-permute-start | bytes 589832 | tf_op jit(solution)/shard_map/while/body/eval_jaxpr/ppermute | solution.py:13
  263.4 4.3 %collective-permute-start.3 = (f32[384,1,128]{2,0,1:T(8,128)S(1)}, f32[384,1,128]{2,0,1:T(8,128)S(1)}, u32[]{:S(2)}, u32[]{:S(2)}) collective-permute-start(f32[384,1,128]{2,0,1:T(8,128)S(1)} %fusion.109), channel_id=1, source_target_pairs={{120,0},{0,8},{8,16},{16,24},{24,32},{32,40},{40,48},{48,56},{56,6... | collective-permute-start | bytes 589832 | tf_op jit(solution)/shard_map/while/body/eval_jaxpr/ppermute | solution.py:13
  268.6 11.8 %collective-permute-start = (bf16[384,128]{1,0:T(8,128)(2,1)S(1)}, bf16[384,128]{1,0:T(8,128)(2,1)}, u32[]{:S(2)}, u32[]{:S(2)}) collective-permute-start(bf16[384,128]{1,0:T(8,128)(2,1)S(1)} %copy.91), channel_id=1, source_target_pairs={{120,0},{0,8},{8,16},{16,24},{24,32},{32,40},{40,48},{48,56},{56,6... | collective-permute-start | bytes 294920 | tf_op jit(solution)/shard_map/while/body/eval_jaxpr/ppermute | solution.py:13
  272.0 8.4 %collective-permute-start.1 = (bf16[384,128]{1,0:T(8,128)(2,1)S(1)}, bf16[384,128]{1,0:T(8,128)(2,1)}, u32[]{:S(2)}, u32[]{:S(2)}) collective-permute-start(bf16[384,128]{1,0:T(8,128)(2,1)S(1)} %copy.92), channel_id=1, source_target_pairs={{120,0},{0,8},{8,16},{16,24},{24,32},{32,40},{40,48},{48,56},{56,6... | collective-permute-start | bytes 294920 | tf_op jit(solution)/shard_map/while/body/eval_jaxpr/ppermute | solution.py:13
  274.6 5.7 %collective-permute-start.2 = (f32[384,1,128]{2,0,1:T(8,128)}, f32[384,1,128]{2,0,1:T(8,128)S(1)}, u32[]{:S(2)}, u32[]{:S(2)}) collective-permute-start(f32[384,1,128]{2,0,1:T(8,128)} %fusion.108), channel_id=1, source_target_pairs={{120,0},{0,8},{8,16},{16,24},{24,32},{32,40},{40,48},{48,56},{56,6... | collective-permute-start | bytes 589832 | tf_op jit(solution)/shard_map/while/body/eval_jaxpr/ppermute | solution.py:13
  277.4 4.3 %collective-permute-start.3 = (f32[384,1,128]{2,0,1:T(8,128)S(1)}, f32[384,1,128]{2,0,1:T(8,128)S(1)}, u32[]{:S(2)}, u32[]{:S(2)}) collective-permute-start(f32[384,1,128]{2,0,1:T(8,128)S(1)} %fusion.109), channel_id=1, source_target_pairs={{120,0},{0,8},{8,16},{16,24},{24,32},{32,40},{40,48},{48,56},{56,6... | collective-permute-start | bytes 589832 | tf_op jit(solution)/shard_map/while/body/eval_jaxpr/ppermute | solution.py:13
  282.5 11.8 %collective-permute-start = (bf16[384,128]{1,0:T(8,128)(2,1)S(1)}, bf16[384,128]{1,0:T(8,128)(2,1)}, u32[]{:S(2)}, u32[]{:S(2)}) collective-permute-start(bf16[384,128]{1,0:T(8,128)(2,1)S(1)} %copy.91), channel_id=1, source_target_pairs={{120,0},{0,8},{8,16},{16,24},{24,32},{32,40},{40,48},{48,56},{56,6... | collective-permute-start | bytes 294920 | tf_op jit(solution)/shard_map/while/body/eval_jaxpr/ppermute | solution.py:13
  285.9 8.4 %collective-permute-start.1 = (bf16[384,128]{1,0:T(8,128)(2,1)S(1)}, bf16[384,128]{1,0:T(8,128)(2,1)}, u32[]{:S(2)}, u32[]{:S(2)}) collective-permute-start(bf16[384,128]{1,0:T(8,128)(2,1)S(1)} %copy.92), channel_id=1, source_target_pairs={{120,0},{0,8},{8,16},{16,24},{24,32},{32,40},{40,48},{48,56},{56,6... | collective-permute-start | bytes 294920 | tf_op jit(solution)/shard_map/while/body/eval_jaxpr/ppermute | solution.py:13
  288.6 5.7 %collective-permute-start.2 = (f32[384,1,128]{2,0,1:T(8,128)}, f32[384,1,128]{2,0,1:T(8,128)S(1)}, u32[]{:S(2)}, u32[]{:S(2)}) collective-permute-start(f32[384,1,128]{2,0,1:T(8,128)} %fusion.108), channel_id=1, source_target_pairs={{120,0},{0,8},{8,16},{16,24},{24,32},{32,40},{40,48},{48,56},{56,6... | collective-permute-start | bytes 589832 | tf_op jit(solution)/shard_map/while/body/eval_jaxpr/ppermute | solution.py:13
  296.5 11.8 %collective-permute-start = (bf16[384,128]{1,0:T(8,128)(2,1)S(1)}, bf16[384,128]{1,0:T(8,128)(2,1)}, u32[]{:S(2)}, u32[]{:S(2)}) collective-permute-start(bf16[384,128]{1,0:T(8,128)(2,1)S(1)} %copy.91), channel_id=1, source_target_pairs={{120,0},{0,8},{8,16},{16,24},{24,32},{32,40},{40,48},{48,56},{56,6... | collective-permute-start | bytes 294920 | tf_op jit(solution)/shard_map/while/body/eval_jaxpr/ppermute | solution.py:13
  299.9 8.4 %collective-permute-start.1 = (bf16[384,128]{1,0:T(8,128)(2,1)S(1)}, bf16[384,128]{1,0:T(8,128)(2,1)}, u32[]{:S(2)}, u32[]{:S(2)}) collective-permute-start(bf16[384,128]{1,0:T(8,128)(2,1)S(1)} %copy.92), channel_id=1, source_target_pairs={{120,0},{0,8},{8,16},{16,24},{24,32},{32,40},{40,48},{48,56},{56,6... | collective-permute-start | bytes 294920 | tf_op jit(solution)/shard_map/while/body/eval_jaxpr/ppermute | solution.py:13
  302.6 5.7 %collective-permute-start.2 = (f32[384,1,128]{2,0,1:T(8,128)}, f32[384,1,128]{2,0,1:T(8,128)S(1)}, u32[]{:S(2)}, u32[]{:S(2)}) collective-permute-start(f32[384,1,128]{2,0,1:T(8,128)} %fusion.108), channel_id=1, source_target_pairs={{120,0},{0,8},{8,16},{16,24},{24,32},{32,40},{40,48},{48,56},{56,6... | collective-permute-start | bytes 589832 | tf_op jit(solution)/shard_map/while/body/eval_jaxpr/ppermute | solution.py:13
  319.3 33.0 %reduce-scatter.5.cloned.1.call-start = ((), (), s32[]{:S(2)}) async-start(), calls=%async_computation.4 | async-start | bytes 147456 | tf_op jit(solution)/shard_map/reduce_scatter | solution.py:120
  (12 other events, 42.5 us)
Sparse Core Ops, SparseCore 0:
  10.4 36.6 all-gather.1
  319.4 16.5 reduce-scatter.2
  338.9 13.4 reduce-scatter.4
where the time goes:
time: 361 us; the launch traced here: 359 us
  matrix products  126 us (35%)
  waiting for transfers between devices  82.3 us (23%)
  starting transfers between devices  73 us (20%)
  local copies, waits for them, and re-layouts  39.4 us (11%)
  other arithmetic  23.5 us (7%)
  between operations  13.9 us (4%)
    ppermute x64, starting transfers between devices, from_behind(): return lax.ppermute(block, axis, route)  72.9 us
    dot_general x16, matrix products, attend_back(): jnp.einsum('tgnp,pgd->tgnd', grad_score, key_heads, preferred_element_typ...  44.2 us
    all_gather x1, waiting for transfers between devices, shards(): shard_piece = lax.all_gather(key_prompt, 'blk', axis=0, tiled=True)  30.1 us
    while x32, local copies, waits for them, and re-layouts  28.6 us
    ppermute x64, waiting for transfers between devices, from_behind(): return lax.ppermute(block, axis, route)  22.1 us
    dot_general x1, matrix products, shards(): jnp.einsum('tgnd,pgd->tgnp', query_heads, piece_keys, preferred_element_t...  20.7 us
    dot_general x16, matrix products, attend_back(): jnp.einsum('tgnp,tgnd->pgd', grad_score, query_heads, preferred_element_t...  20.2 us
    reduce_sum x1, other arithmetic, shards(): new_total = start_total * jnp.exp(start_max - new_max) + jnp.exp(scores -...  20.1 us
  transfers between devices with their start and end apart: 67, of which 20 were waited for; matrix products, arithmetic and copies ran while one was open for 33% of the time, Pallas kernels for 0%

commit v1 on v0

v1 whole, which is shorter than its diff:
```python
import functools

import jax
import jax.numpy as jnp
from jax import lax
from jax.experimental import pallas as pl
from jax.experimental.pallas import tpu as pltpu
from jax.sharding import PartitionSpec as P

HD = 128
GROUP = 8
CTOK = 256
ROWS = 384
TILE = 2 * ROWS
X, Y, CORES = 4, 4, 2
SCALE = HD ** (-0.5)
EXP2_SCALE = SCALE * 1.4426950408889634
VMEM_LIMIT = 56 * 1024 * 1024
F32 = jnp.float32
BF16 = jnp.bfloat16


def place(x, y, core):
    return ((x * 2 + y % 2) * CORES + core) * 2 + y // 2


def send(block, dx=0, dy=0, dc=0):
    route = []
    for x in range(X):
        for y in range(Y):
            for core in range(CORES):
                there = place((x + dx) % X, (y + dy) % Y, core ^ dc)
                route.append((place(x, y, core), there))
    return lax.ppermute(block, ("blk", "req"), route)


def head(ref, n, width):
    return ref[:, n * width : (n + 1) * width]


def dot(a, b, contract):
    return lax.dot_general(a, b, (contract, ((), ())), preferred_element_type=F32)


def fold_scores(scores, n, m_ref, l_ref, e_ref, mt_ref):
    m_old = m_ref[n : n + 1, :]
    m_new = jnp.maximum(m_old, jnp.max(scores, axis=0, keepdims=True))
    e = jnp.exp2(scores - m_new)
    total = jnp.sum(e, axis=0, keepdims=True)
    l_ref[n : n + 1, :] = l_ref[n : n + 1, :] * jnp.exp2(m_old - m_new) + total
    m_ref[n : n + 1, :] = m_new
    mt_ref[0, n : n + 1, :] = m_new
    e_ref[:, n * CTOK : (n + 1) * CTOK] = e.astype(BF16)


def self_scores_kernel(q_ref, k_ref, out_ref, do_ref, col_ref, row_ref, e_ref, mt_ref, m_ref, l_ref, d_ref):
    keys = k_ref[...]
    visible = col_ref[...] <= row_ref[...]
    m_ref[...] = jnp.full((GROUP, CTOK), -1e30, F32)
    l_ref[...] = jnp.zeros((GROUP, CTOK), F32)
    for n in range(GROUP):
        product = head(do_ref, n, HD).astype(F32) * head(out_ref, n, HD).astype(F32)
        d_ref[n : n + 1, :] = jnp.sum(product.T, axis=0, keepdims=True)
        scores = dot(keys, head(q_ref, n, HD), ((1,), (1,))) * EXP2_SCALE
        scores = jnp.where(visible, scores, -jnp.inf)
        fold_scores(scores, n, m_ref, l_ref, e_ref, mt_ref)


def prompt_scores_kernel(q_ref, k_ref, m_in, l_in, e_ref, mt_ref, m_ref, l_ref):
    @pl.when(pl.program_id(0) == 0)
    def _():
        m_ref[...] = m_in[...]
        l_ref[...] = l_in[...]

    keys = k_ref[...]
    for n in range(GROUP):
        scores = dot(keys, head(q_ref, n, HD), ((1,), (1,))) * EXP2_SCALE
        fold_scores(scores, n, m_ref, l_ref, e_ref, mt_ref)


def back_tile(keys, values, q_ref, do_ref, e_ref, mt_ref, log_total, d_ref, dq_ref):
    grad_keys = None
    for n in range(GROUP):
        weight = jnp.exp2(mt_ref[0, n : n + 1, :] - log_total[n : n + 1, :])
        probs = head(e_ref, n, CTOK).astype(F32) * weight
        do_n, q_n = head(do_ref, n, HD), head(q_ref, n, HD)
        grad_prob = dot(values, do_n, ((1,), (1,)))
        grad_score = (probs * (grad_prob - d_ref[n : n + 1, :])).astype(BF16)
        part_value = dot(probs.astype(BF16), do_n, ((1,), (0,)))
        part_key = dot(grad_score, q_n, ((1,), (0,)))
        dq_ref[n] += dot(keys, grad_score, ((0,), (0,)))
        if grad_keys is None:
            grad_keys, grad_values = part_key, part_value
        else:
            grad_keys, grad_values = grad_keys + part_key, grad_values + part_value
    return grad_keys * SCALE, grad_values


def prompt_back_kernel(first, *refs):
    if first:
        q_ref, do_ref, kv_ref, e_ref, mt_ref, m_ref, l_ref, d_ref, here_ref, there_ref, dq_ref = refs
    else:
        q_ref, do_ref, kv_ref, e_ref, mt_ref, m_ref, l_ref, d_ref, dq_in, here_ref, there_ref, dq_ref = refs

    @pl.when(pl.program_id(0) == 0)
    def _():
        dq_ref[...] = jnp.zeros_like(dq_ref) if first else dq_in[...]

    log_total = m_ref[...] + jnp.log2(l_ref[...])
    grad_keys, grad_values = back_tile(
        kv_ref[:, :HD], kv_ref[:, HD:], q_ref, do_ref, e_ref, mt_ref, log_total, d_ref, dq_ref
    )
    here_ref[:, :HD] = grad_keys[:ROWS]
    here_ref[:, HD:] = grad_values[:ROWS]
    there_ref[:, :HD] = grad_keys[ROWS:].astype(BF16)
    there_ref[:, HD:] = grad_values[ROWS:].astype(BF16)


def self_back_kernel(q_ref, do_ref, k_ref, v_ref, e_ref, mt_ref, m_ref, l_ref, d_ref, dq_in, dk_ref, dv_ref, out_ref, dq_ref):
    dq_ref[...] = dq_in[...]
    log_total = m_ref[...] + jnp.log2(l_ref[...])
    grad_keys, grad_values = back_tile(
        k_ref[...], v_ref[...], q_ref, do_ref, e_ref, mt_ref, log_total, d_ref, dq_ref
    )
    dk_ref[...] = grad_keys.astype(BF16)
    dv_ref[...] = grad_values.astype(BF16)
    for n in range(GROUP):
        out_ref[:, n * HD : (n + 1) * HD] = (dq_ref[n] * SCALE).T.astype(BF16)


def whole(shape):
    return pl.BlockSpec(shape, lambda *_: (0,) * len(shape))


PARAMS = pltpu.CompilerParams(vmem_limit_bytes=VMEM_LIMIT)
STAT = (GROUP, CTOK)
WIDE = GROUP * CTOK
DQ = (GROUP, HD, CTOK)


def cost(rows, matmuls, exps, stored):
    return pl.CostEstimate(
        flops=2 * 2 * rows * WIDE * HD * matmuls,
        bytes_accessed=rows * WIDE * 2 * stored,
        transcendentals=rows * WIDE * exps,
    )


def self_scores(query, key_comp, out, d_out, col, row):
    return pl.pallas_call(
        self_scores_kernel,
        out_shape=(
            jax.ShapeDtypeStruct((CTOK, WIDE), BF16),
            jax.ShapeDtypeStruct((1,) + STAT, F32),
            jax.ShapeDtypeStruct(STAT, F32),
            jax.ShapeDtypeStruct(STAT, F32),
            jax.ShapeDtypeStruct(STAT, F32),
        ),
        compiler_params=PARAMS,
        cost_estimate=cost(CTOK, 1, 1, 1),
        name="self_scores",
    )(query, key_comp, out, d_out, col, row)


def prompt_scores(query, kv, m, l):
    tiles = kv.shape[0] // TILE
    return pl.pallas_call(
        prompt_scores_kernel,
        grid=(tiles,),
        in_specs=[
            whole((CTOK, GROUP * HD)),
            pl.BlockSpec((TILE, HD), lambda t: (t, 0)),
            whole(STAT),
            whole(STAT),
        ],
        out_specs=(
            pl.BlockSpec((TILE, WIDE), lambda t: (t, 0)),
            pl.BlockSpec((1,) + STAT, lambda t: (t, 0, 0)),
            whole(STAT),
            whole(STAT),
        ),
        out_shape=(
            jax.ShapeDtypeStruct((tiles * TILE, WIDE), BF16),
            jax.ShapeDtypeStruct((tiles,) + STAT, F32),
            jax.ShapeDtypeStruct(STAT, F32),
            jax.ShapeDtypeStruct(STAT, F32),
        ),
        compiler_params=PARAMS,
        cost_estimate=cost(tiles * TILE, 1, 1, 1),
        name="prompt_scores",
    )(query, kv, m, l)


def prompt_back(query, d_out, kv, e, mt, m, l, d, dq):
    tiles = kv.shape[0] // TILE
    first = dq is None
    return pl.pallas_call(
        functools.partial(prompt_back_kernel, first),
        grid=(tiles,),
        in_specs=[
            whole((CTOK, GROUP * HD)),
            whole((CTOK, GROUP * HD)),
            pl.BlockSpec((TILE, 2 * HD), lambda t: (t, 0)),
            pl.BlockSpec((TILE, WIDE), lambda t: (t, 0)),
            pl.BlockSpec((1,) + STAT, lambda t: (t, 0, 0)),
            whole(STAT),
            whole(STAT),
            whole(STAT),
        ]
        + ([] if first else [whole(DQ)]),
        out_specs=(
            pl.BlockSpec((ROWS, 2 * HD), lambda t: (t, 0)),
            pl.BlockSpec((ROWS, 2 * HD), lambda t: (t, 0)),
            whole(DQ),
        ),
        out_shape=(
            jax.ShapeDtypeStruct((tiles * ROWS, 2 * HD), F32),
            jax.ShapeDtypeStruct((tiles * ROWS, 2 * HD), BF16),
            jax.ShapeDtypeStruct(DQ, F32),
        ),
        compiler_params=PARAMS,
        cost_estimate=cost(tiles * TILE, 4, 0, 1),
        name="prompt_back",
    )(query, d_out, kv, e, mt, m, l, d, *([] if first else [dq]))


def self_back(query, d_out, key_comp, value_comp, e, mt, m, l, d, dq):
    return pl.pallas_call(
        self_back_kernel,
        out_shape=(
            jax.ShapeDtypeStruct((CTOK, HD), BF16),
            jax.ShapeDtypeStruct((CTOK, HD), BF16),
            jax.ShapeDtypeStruct((CTOK, GROUP * HD), BF16),
        ),
        scratch_shapes=[pltpu.VMEM(DQ, F32)],
        compiler_params=PARAMS,
        cost_estimate=cost(CTOK, 4, 0, 1),
        name="self_back",
    )(query, d_out, key_comp, value_comp, e, mt, m, l, d, dq)


def shards(query, key_comp, value_comp, key_prompt, value_prompt, out, d_out, steps):
    here = jnp.concatenate([key_prompt, value_prompt], axis=1)
    low, high = slice(0, ROWS // 2), slice(ROWS // 2, ROWS)

    beside = send(here, dc=1)
    left = send(here, dx=1)
    right = send(here, dx=-1)
    here_y = send(here, dy=1)
    far_low = send(left[low], dx=1)
    far_high = send(right[high], dx=-1)
    left_y = send(left, dy=1)
    right_y = send(right, dy=-1)
    far = jnp.concatenate([far_low, far_high], axis=0)
    far_y = send(far, dy=-1)
    near = jnp.concatenate([here, beside, here_y, send(here_y, dc=1)], axis=0)
    sides = jnp.concatenate(
        [right, send(right, dc=1), right_y, send(right_y, dc=1), left, send(left, dc=1), left_y, send(left_y, dc=1)],
        axis=0,
    )
    opposite = jnp.concatenate([far, send(far, dc=1), far_y, send(far_y, dc=1)], axis=0)

    e_self, mt_self, m, l, d = self_scores(
        query, key_comp, out, d_out, steps.reshape(CTOK, 1), steps.reshape(1, CTOK)
    )
    e_near, mt_near, m, l = prompt_scores(query, near, m, l)
    e_sides, mt_sides, m, l = prompt_scores(query, sides, m, l)
    e_opposite, mt_opposite, m, l = prompt_scores(query, opposite, m, l)

    back = functools.partial(prompt_back, query, d_out)
    mine, theirs, dq = back(opposite, e_opposite, mt_opposite, m, l, d, None)
    total = mine + send(theirs, dc=1).astype(F32)
    total_low = send(total[:, :HD].astype(BF16), dx=1)
    total_high = send(total[:, HD:].astype(BF16), dx=-1)

    mine, theirs, dq = back(sides, e_sides, mt_sides, m, l, d, dq)
    total = mine + send(theirs, dc=1).astype(F32)
    to_right = jnp.concatenate([total[:TILE, :HD] + total_low.astype(F32), total[:TILE, HD:]], axis=1)
    to_left = jnp.concatenate([total[TILE:, :HD], total[TILE:, HD:] + total_high.astype(F32)], axis=1)
    from_left = send(to_right.astype(BF16), dx=1)
    from_right = send(to_left.astype(BF16), dx=-1)

    mine, theirs, dq = back(near, e_near, mt_near, m, l, d, dq)
    total = mine + send(theirs, dc=1).astype(F32) + from_left.astype(F32) + from_right.astype(F32)
    grad_key_comp, grad_value_comp, grad_query = self_back(
        query, d_out, key_comp, value_comp, e_self, mt_self, m, l, d, dq
    )

    total = total.reshape(2, 2, ROWS // 2, 2 * HD)
    y_high = lax.axis_index("req")
    y_low = (lax.axis_index("blk") // CORES) % 2
    up = y_high ^ y_low
    pick = lambda rows, half: lax.dynamic_index_in_dim(rows, half, 0, keepdims=False)
    across = send(pick(total[0], 1 - y_high).astype(BF16), dy=2)
    above = send(pick(total[1], up).astype(BF16), dy=1)
    below = send(pick(total[1], 1 - up).astype(BF16), dy=-1)
    total = pick(total[0], y_high) + across.astype(F32) + above.astype(F32) + below.astype(F32)
    return (
        grad_query,
        grad_key_comp,
        grad_value_comp,
        total[:, :HD].astype(BF16),
        total[:, HD:].astype(BF16),
    )


def solution(mesh):
    rows = P(("blk", "req"), "head")
    return jax.shard_map(
        shards,
        mesh=mesh,
        in_specs=(rows, rows, rows, P("blk", "head"), P("blk", "head"), rows, rows, P(("blk", "req"))),
        out_specs=(rows,) * 5,
        check_vma=False,
    )
```

time: 361 us -> 135 us (0.37)
  matrix products: 126 us -> 0 us
  Pallas kernels: 0 us -> 76.3 us
  waiting for transfers between devices: 82.3 us -> 20 us
  starting transfers between devices: 73 us -> 26.9 us
  local copies, waits for them, and re-layouts: 39.4 us -> 6.35 us
  other arithmetic: 23.5 us -> 1.76 us
  between operations: 13.9 us -> 0.99 us
    dot_general x86 -> x0, matrix products: 126 us -> none  [the longest x16 44.2 us: attend_back(): jnp.einsum('tgnp,pgd->tgnd', grad_score, key_heads, preferred_element_typ...]
    pallas_call x0 -> x8, Pallas kernels: none -> 76.3 us  [the longest x3 42.3 us: prompt_back(): pl.pallas_call(functools.partial(prompt_back_kernel, first), grid=(tiles,...]
    ppermute x64 -> x26, starting transfers between devices: 72.9 us -> 26.9 us  [send(): return lax.ppermute(block, ('blk', 'req'), route)]
    while x33 -> x0, local copies, waits for them, and re-layouts: 31.3 us -> none
    all_gather x1 -> x0, waiting for transfers between devices: 30.1 us -> none  [shards(): shard_piece = lax.all_gather(key_prompt, 'blk', axis=0, tiled=True)]
    reduce_scatter x2 -> x0, waiting for transfers between devices: 30 us -> none  [the longest x1 16.4 us: shards(): lax.psum_scatter(value_acc.reshape(shard_rows, -1).astype(jnp.bfloat16),...]
    reduce_sum x3 -> x0, other arithmetic: 20.7 us -> none  [the longest x1 20.1 us: shards(): new_total = start_total * jnp.exp(start_max - new_max) + jnp.exp(scores -...]
    unnamed x27 -> x23, local copies, waits for them, and re-layouts: 8.05 us -> 3.12 us
  transfers between devices with their start and end apart: 67 -> 26, of which waited for: 20 -> 6; matrix products, arithmetic and copies ran while one was open for 33% -> 2% of each run, Pallas kernels for 0% -> 29%
where the time goes in v1:
time: 135 us; the launch traced here: 132 us
  Pallas kernels  76.3 us (57%)
  starting transfers between devices  26.9 us (20%)
  waiting for transfers between devices  20 us (15%)
  local copies, waits for them, and re-layouts  6.35 us (5%)
  other arithmetic  1.76 us (1%)
    pallas_call x3, Pallas kernels, prompt_back(): pl.pallas_call(functools.partial(prompt_back_kernel, first), grid=(tiles,...  42.3 us
    ppermute x26, starting transfers between devices, send(): return lax.ppermute(block, ('blk', 'req'), route)  26.9 us
    pallas_call x3, Pallas kernels, prompt_scores(): pl.pallas_call(prompt_scores_kernel, grid=(tiles,), in_specs=[whole((CTOK...  25.9 us
    ppermute x26, waiting for transfers between devices, send(): return lax.ppermute(block, ('blk', 'req'), route)  20 us
    pallas_call x1, Pallas kernels, self_back(): pl.pallas_call(self_back_kernel, out_shape=(jax.ShapeDtypeStruct((CTOK, H...  4.85 us
    pallas_call x1, Pallas kernels, self_scores(): pl.pallas_call(self_scores_kernel, out_shape=(jax.ShapeDtypeStruct((CTOK,...  3.3 us
    unnamed x23, local copies, waits for them, and re-layouts  3.12 us
  transfers between devices with their start and end apart: 26, of which 6 were waited for; matrix products, arithmetic and copies ran while one was open for 2% of the time, Pallas kernels for 29%

profile of v1, /device:TPU:1, one launch (start us, length us, event | category | flops | bytes accessed | tf_op | source)
XLA Modules:
  0.0 132.3 jit_solution(5928281690789801092)
XLA Ops:
  0.6 0.9 constant_dynamic-update-slice_fusion.1
  1.5 0.9 constant_dynamic-update-slice_fusion
  2.5 2.1 %collective-permute-start = (bf16[384,256]{1,0:T(8,128)(2,1)S(1)}, bf16[384,256]{1,0:T(8,128)(2,1)S(1)}, u32[]{:S(2)}, u32[]{:S(2)}) collective-permute-start(bf16[384,256]{1,0:T(8,128)(2,1)S(1)} %constant_dynamic-update-slice_fusion), channel_id=1, source_target_pairs={{0,32},{8,40},{16,48},{24,56},{4,36},{12,44},{20,52},{28,60},{32,6... | collective-permute-start | bytes 589832 | tf_op jit(solution)/shard_map/ppermute | solution.py:34
  4.6 1.3 %collective-permute-start.2 = (bf16[384,256]{1,0:T(8,128)(2,1)S(1)}, bf16[384,256]{1,0:T(8,128)(2,1)S(1)}, u32[]{:S(2)}, u32[]{:S(2)}) collective-permute-start(bf16[384,256]{1,0:T(8,128)(2,1)S(1)} %constant_dynamic-update-slice_fusion), channel_id=1, source_target_pairs={{0,96},{8,104},{16,112},{24,120},{4,100},{12,108},{20,116},{28,124... | collective-permute-start | bytes 589832 | tf_op jit(solution)/shard_map/ppermute | solution.py:34
  5.9 1.4 %collective-permute-start.14 = (bf16[384,256]{1,0:T(8,128)(2,1)S(1)}, bf16[384,256]{1,0:T(8,128)(2,1)S(1)}, u32[]{:S(2)}, u32[]{:S(2)}) collective-permute-start(bf16[384,256]{1,0:T(8,128)(2,1)S(1)} %constant_dynamic-update-slice_fusion), channel_id=1, source_target_pairs={{0,16},{8,24},{16,4},{24,12},{4,20},{12,28},{20,0},{28,8},{32,48},... | collective-permute-start | bytes 589832 | tf_op jit(solution)/shard_map/ppermute | solution.py:34
  7.3 1.5 %collective-permute-start.13 = (bf16[384,256]{1,0:T(8,128)(2,1)S(1)}, bf16[384,256]{1,0:T(8,128)(2,1)S(1)}, u32[]{:S(2)}, u32[]{:S(2)}) collective-permute-start(bf16[384,256]{1,0:T(8,128)(2,1)S(1)} %constant_dynamic-update-slice_fusion), channel_id=1, source_target_pairs={{0,8},{8,0},{16,24},{24,16},{4,12},{12,4},{20,28},{28,20},{32,40},... | collective-permute-start | bytes 589832 | tf_op jit(solution)/shard_map/ppermute | solution.py:34
  8.9 1.5 %copy.13.col_ref = s32[256,1]{1,0:T(8,128)} copy(s32[256,1]{0,1:T(1,128)} %bitcast.21) | data formatting | bytes 2048 | tf_op jit(solution)/shard_map/reshape | solution.py:264
  10.3 3.3 %self_scores.1 = (bf16[256,2048]{1,0:T(8,128)(2,1)}, f32[1,8,256]{2,1,0:T(8,128)}, f32[8,256]{1,0:T(8,128)}, f32[8,256]{1,0:T(8,128)}, f32[8,256]{1,0:T(8,128)}) custom-call(bf16[256,1024]{1,0:T(8,128)(2,1)} %q_ref.9, bf16[256,128]{1,0:T(8,128)(2,1)} %k_ref.3, bf16[256,1024]{1,0:T(8,128)(2,1)} %out_ref.1, bf16[256,1024]{1,0:T(8,128)(2,1)} %do_ref.3, ...), custom_call_target="tpu_custom_call" | custom-call | flops 268435456 | bytes 1048576 | tf_op jit(solution)/shard_map/self_scores/pallas_call | solution.py:150
  13.6 0.1 collective-permute-start.1
  13.7 0.0 collective-permute-done.2
  13.8 2.7 %collective-permute-start.3 = (bf16[192,256]{1,0:T(8,128)(2,1)S(1)}, bf16[192,256]{1,0:T(8,128)(2,1)S(1)}, u32[]{:S(2)}, u32[]{:S(2)}) collective-permute-start(bf16[192,256]{1,0:T(8,128)(2,1)S(1)} %slice.59), channel_id=1, source_target_pairs={{0,96},{8,104},{16,112},{24,120},{4,100},{12,108},{20,116},{28,124... | collective-permute-start | bytes 294920 | tf_op jit(solution)/shard_map/ppermute | solution.py:34
  16.5 0.6 collective-permute-start.7
  17.1 2.3 %collective-permute-done.1 = bf16[192,256]{1,0:T(8,128)(2,1)S(1)} collective-permute-done((bf16[192,256]{1,0:T(8,128)(2,1)S(1)}, bf16[192,256]{1,0:T(8,128)(2,1)S(1)}, u32[]{:S(2)}, u32[]{:S(2)}) %collective-permute-start.1) | collective-permute-done | bytes 98336 | tf_op jit(solution)/shard_map/ppermute | solution.py:34
  19.4 1.3 collective-permute-start.8
  20.7 1.1 collective-permute-start.10
  21.8 0.0 collective-permute-done.14
  21.8 0.2 collective-permute-start.11
  22.1 0.0 collective-permute-done.7
  22.1 0.3 collective-permute-start.15
  22.4 2.6 %collective-permute-done.8 = bf16[384,256]{1,0:T(8,128)(2,1)S(1)} collective-permute-done((bf16[384,256]{1,0:T(8,128)(2,1)S(1)}, bf16[384,256]{1,0:T(8,128)(2,1)S(1)}, u32[]{:S(2)}, u32[]{:S(2)}) %collective-permute-start.8) | collective-permute-done | bytes 196640 | tf_op jit(solution)/shard_map/ppermute | solution.py:34
  25.0 1.7 %collective-permute-start.4 = (bf16[384,256]{1,0:T(8,128)(2,1)S(1)}, bf16[384,256]{1,0:T(8,128)(2,1)S(1)}, u32[]{:S(2)}, u32[]{:S(2)}) collective-permute-start(bf16[384,256]{1,0:T(8,128)(2,1)S(1)} %get-tuple-element.75), channel_id=1, source_target_pairs={{0,8},{8,0},{16,24},{24,16},{4,12},{12,4},{20,28},{28,20},{32,40},... | collective-permute-start | bytes 589832 | tf_op jit(solution)/shard_map/ppermute | solution.py:34
  26.7 0.0 collective-permute-done.13
  26.7 2.6 %collective-permute-start.5 = (bf16[384,256]{1,0:T(8,128)(2,1)S(1)}, bf16[384,256]{1,0:T(8,128)(2,1)S(1)}, u32[]{:S(2)}, u32[]{:S(2)}) collective-permute-start(bf16[384,256]{1,0:T(8,128)(2,1)S(1)} %get-tuple-element.75), channel_id=1, source_target_pairs={{0,20},{8,28},{16,0},{24,8},{4,16},{12,24},{20,4},{28,12},{32,52},... | collective-permute-start | bytes 589832 | tf_op jit(solution)/shard_map/ppermute | solution.py:34
  29.3 0.4 collective-permute-done.11
  29.6 0.8 collective-permute-start.9
  30.4 0.0 collective-permute-done.15
  30.4 0.0 collective-permute-start.12
  30.5 1.0 pad_maximum_fusion.k_ref.refs_2_
  31.5 7.1 %prompt_scores.3 = (bf16[1536,2048]{1,0:T(8,128)(2,1)}, f32[2,8,256]{2,1,0:T(8,128)}, f32[8,256]{1,0:T(8,128)}, f32[8,256]{1,0:T(8,128)}) custom-call(bf16[256,1024]{1,0:T(8,128)(2,1)} %q_ref.9, bf16[1536,256]{1,0:T(8,128)(2,1)} %pad_maximum_fusion.k_ref.refs_2_, f32[8,256]{1,0:T(8,128)} %get-tuple-element.36.m_in, f32[8,256]{1,0:T(8,128)} %get-tuple-element.37.l_in), custom_call_target="tpu_custom_call" | custom-call | flops 1610612736 | bytes 6291456 | tf_op jit(solution)/shard_map/prompt_scores/pallas_call | solution.py:167
  38.6 0.0 collective-permute-done.5
  38.6 0.7 collective-permute-start.6
  39.4 0.0 collective-permute-done.4
  39.5 0.0 collective-permute-done.10
  39.5 0.0 collective-permute-done.12
  39.6 1.2 copy-done.3
  40.7 11.6 %prompt_scores.4 = (bf16[3072,2048]{1,0:T(8,128)(2,1)}, f32[4,8,256]{2,1,0:T(8,128)}, f32[8,256]{1,0:T(8,128)}, f32[8,256]{1,0:T(8,128)}) custom-call(bf16[256,1024]{1,0:T(8,128)(2,1)} %q_ref.9, bf16[3072,256]{1,0:T(8,128)(2,1)} %copy-done.3, f32[8,256]{1,0:T(8,128)} %get-tuple-element.38.m_in, f32[8,256]{1,0:T(8,128)} %get-tuple-element.39.l_in), custom_call_target="tpu_custom_call" | custom-call | flops 3221225472 | bytes 12582912 | tf_op jit(solution)/shard_map/prompt_scores/pallas_call | solution.py:167
  52.3 0.0 collective-permute-done.6
  52.3 0.9 copy-done.4
  53.2 7.2 %prompt_scores.5 = (bf16[1536,2048]{1,0:T(8,128)(2,1)}, f32[2,8,256]{2,1,0:T(8,128)}, f32[8,256]{1,0:T(8,128)}, f32[8,256]{1,0:T(8,128)}) custom-call(bf16[256,1024]{1,0:T(8,128)(2,1)} %q_ref.9, bf16[1536,256]{1,0:T(8,128)(2,1)} %copy-done.4, f32[8,256]{1,0:T(8,128)} %get-tuple-element.40.m_in, f32[8,256]{1,0:T(8,128)} %get-tuple-element.41.l_in), custom_call_target="tpu_custom_call" | custom-call | flops 1610612736 | bytes 6291456 | tf_op jit(solution)/shard_map/prompt_scores/pallas_call | solution.py:167
  60.4 11.4 %prompt_back.3 = (f32[768,256]{1,0:T(8,128)}, bf16[768,256]{1,0:T(8,128)(2,1)}, f32[8,128,256]{2,1,0:T(8,128)}) custom-call(bf16[256,1024]{1,0:T(8,128)(2,1)} %q_ref.9, bf16[256,1024]{1,0:T(8,128)(2,1)} %do_ref.3, bf16[1536,256]{1,0:T(8,128)(2,1)} %copy-done.4, bf16[1536,2048]{1,0:T(8,128)(2,1)} %get-tuple-element.49.refs_3_, ...), custom_call_target="tpu_custom_call" | custom-call | flops 6442450944 | bytes 6291456 | tf_op jit(solution)/shard_map/prompt_back/pallas_call | solution.py:197
  71.8 19.0 %prompt_back.4 = (f32[1536,256]{1,0:T(8,128)}, bf16[1536,256]{1,0:T(8,128)(2,1)}, f32[8,128,256]{2,1,0:T(8,128)}) custom-call(bf16[256,1024]{1,0:T(8,128)(2,1)} %q_ref.9, bf16[256,1024]{1,0:T(8,128)(2,1)} %do_ref.3, bf16[3072,256]{1,0:T(8,128)(2,1)} %copy-done.3, bf16[3072,2048]{1,0:T(8,128)(2,1)} %get-tuple-element.47.refs_3_, ...), custom_call_target="tpu_custom_call" | custom-call | flops 12884901888 | bytes 12582912 | tf_op jit(solution)/shard_map/prompt_back/pallas_call | solution.py:197
  90.8 0.1 collective-permute-start.17
  90.9 0.5 collective-permute-start.18
  91.4 11.8 %prompt_back.5 = (f32[768,256]{1,0:T(8,128)}, bf16[768,256]{1,0:T(8,128)(2,1)}, f32[8,128,256]{2,1,0:T(8,128)}) custom-call(bf16[256,1024]{1,0:T(8,128)(2,1)} %q_ref.9, bf16[256,1024]{1,0:T(8,128)(2,1)} %do_ref.3, bf16[1536,256]{1,0:T(8,128)(2,1)} %pad_maximum_fusion.k_ref.refs_2_, bf16[1536,2048]{1,0:T(8,128)(2,1)} %get-tuple-element.45.refs_3_, ...), custom_call_target="tpu_custom_call" | custom-call | flops 6442450944 | bytes 6291456 | tf_op jit(solution)/shard_map/prompt_back/pallas_call | solution.py:197
  103.2 0.4 collective-permute-start.16
  103.6 0.0 collective-permute-done.18
  103.6 0.1 add_convert_fusion
  103.7 0.1 collective-permute-start.19
  103.8 2.7 %collective-permute-start.21 = (bf16[768,128]{1,0:T(8,128)(2,1)S(1)}, bf16[768,128]{1,0:T(8,128)(2,1)S(1)}, u32[]{:S(2)}, u32[]{:S(2)}) collective-permute-start(bf16[768,128]{1,0:T(8,128)(2,1)S(1)} %get-tuple-element.70), channel_id=1, source_target_pairs={{0,96},{8,104},{16,112},{24,120},{4,100},{12,108},{20,116},{28,124... | collective-permute-start | bytes 589832 | tf_op jit(solution)/shard_map/ppermute | solution.py:34
  106.5 0.3 fusion.8
  106.8 4.5 %collective-permute-done.19 = bf16[768,128]{1,0:T(8,128)(2,1)S(1)} collective-permute-done((bf16[768,128]{1,0:T(8,128)(2,1)S(1)}, bf16[768,128]{1,0:T(8,128)(2,1)S(1)}, u32[]{:S(2)}, u32[]{:S(2)}) %collective-permute-start.19) | collective-permute-done | bytes 196640 | tf_op jit(solution)/shard_map/ppermute | solution.py:34
  111.4 0.1 fusion.1
  111.5 2.4 %collective-permute-start.22 = (bf16[768,256]{1,0:T(8,128)(2,1)S(1)}, bf16[768,256]{1,0:T(8,128)(2,1)S(1)}, u32[]{:S(2)}, u32[]{:S(2)}) collective-permute-start(bf16[768,256]{1,0:T(8,128)(2,1)S(1)} %pad_maximum_fusion.2), channel_id=1, source_target_pairs={{0,96},{8,104},{16,112},{24,120},{4,100},{12,108},{20,116},{28,124... | collective-permute-start | bytes 1179656 | tf_op jit(solution)/shard_map/ppermute | solution.py:34
  114.0 0.1 collective-permute-start.20
  114.1 0.0 collective-permute-done.16
  114.1 7.1 %collective-permute-done.22 = bf16[768,256]{1,0:T(8,128)(2,1)S(1)} collective-permute-done((bf16[768,256]{1,0:T(8,128)(2,1)S(1)}, bf16[768,256]{1,0:T(8,128)(2,1)S(1)}, u32[]{:S(2)}, u32[]{:S(2)}) %collective-permute-start.22) | collective-permute-done | bytes 393248 | tf_op jit(solution)/shard_map/ppermute | solution.py:34
  121.2 3.1 %collective-permute-done.20 = bf16[768,256]{1,0:T(8,128)(2,1)S(1)} collective-permute-done((bf16[768,256]{1,0:T(8,128)(2,1)S(1)}, bf16[768,256]{1,0:T(8,128)(2,1)S(1)}, u32[]{:S(2)}, u32[]{:S(2)}) %collective-permute-start.20) | collective-permute-done | bytes 393248 | tf_op jit(solution)/shard_map/ppermute | solution.py:34
  124.3 0.2 convert_add_fusion.1
  124.5 0.5 collective-permute-start.25
  125.0 1.0 collective-permute-start.24
  126.1 0.7 collective-permute-start.23
  126.8 4.9 %self_back.1 = (bf16[256,128]{1,0:T(8,128)(2,1)}, bf16[256,128]{1,0:T(8,128)(2,1)}, bf16[256,1024]{1,0:T(8,128)(2,1)}) custom-call(bf16[256,1024]{1,0:T(8,128)(2,1)} %q_ref.9, bf16[256,1024]{1,0:T(8,128)(2,1)} %do_ref.3, bf16[256,128]{1,0:T(8,128)(2,1)} %k_ref.3, bf16[256,128]{1,0:T(8,128)(2,1)} %v_ref.1, bf16[256,2048]{1,0:T(8,128)(2,1)} %get-tuple-element.34.e_ref, ...), custom_call_target="tpu_custom_call" | custom-call | flops 1073741824 | bytes 1048576 | tf_op jit(solution)/shard_map/self_back/pallas_call | solution.py:228
  131.6 0.1 fusion.4
  131.7 0.6 fusion.11
  (41 shorter events, 0.5 us)
Async XLA Ops:
  2.5 11.2 %collective-permute-start = (bf16[384,256]{1,0:T(8,128)(2,1)S(1)}, bf16[384,256]{1,0:T(8,128)(2,1)S(1)}, u32[]{:S(2)}, u32[]{:S(2)}) collective-permute-start(bf16[384,256]{1,0:T(8,128)(2,1)S(1)} %constant_dynamic-update-slice_fusion), channel_id=1, source_target_pairs={{0,32},{8,40},{16,48},{24,56},{4,36},{12,44},{20,52},{28,60},{32,6... | collective-permute-start | bytes 589832 | tf_op jit(solution)/shard_map/ppermute | solution.py:34
  4.6 9.2 %collective-permute-start.2 = (bf16[384,256]{1,0:T(8,128)(2,1)S(1)}, bf16[384,256]{1,0:T(8,128)(2,1)S(1)}, u32[]{:S(2)}, u32[]{:S(2)}) collective-permute-start(bf16[384,256]{1,0:T(8,128)(2,1)S(1)} %constant_dynamic-update-slice_fusion), channel_id=1, source_target_pairs={{0,96},{8,104},{16,112},{24,120},{4,100},{12,108},{20,116},{28,124... | collective-permute-start | bytes 589832 | tf_op jit(solution)/shard_map/ppermute | solution.py:34
  5.9 15.9 %collective-permute-start.14 = (bf16[384,256]{1,0:T(8,128)(2,1)S(1)}, bf16[384,256]{1,0:T(8,128)(2,1)S(1)}, u32[]{:S(2)}, u32[]{:S(2)}) collective-permute-start(bf16[384,256]{1,0:T(8,128)(2,1)S(1)} %constant_dynamic-update-slice_fusion), channel_id=1, source_target_pairs={{0,16},{8,24},{16,4},{24,12},{4,20},{12,28},{20,0},{28,8},{32,48},... | collective-permute-start | bytes 589832 | tf_op jit(solution)/shard_map/ppermute | solution.py:34
  7.3 19.4 %collective-permute-start.13 = (bf16[384,256]{1,0:T(8,128)(2,1)S(1)}, bf16[384,256]{1,0:T(8,128)(2,1)S(1)}, u32[]{:S(2)}, u32[]{:S(2)}) collective-permute-start(bf16[384,256]{1,0:T(8,128)(2,1)S(1)} %constant_dynamic-update-slice_fusion), channel_id=1, source_target_pairs={{0,8},{8,0},{16,24},{24,16},{4,12},{12,4},{20,28},{28,20},{32,40},... | collective-permute-start | bytes 589832 | tf_op jit(solution)/shard_map/ppermute | solution.py:34
  13.6 5.7 %collective-permute-start.1 = (bf16[192,256]{1,0:T(8,128)(2,1)S(1)}, bf16[192,256]{1,0:T(8,128)(2,1)S(1)}, u32[]{:S(2)}, u32[]{:S(2)}) collective-permute-start(bf16[192,256]{1,0:T(8,128)(2,1)S(1)} %slice.58), channel_id=1, source_target_pairs={{0,32},{8,40},{16,48},{24,56},{4,36},{12,44},{20,52},{28,60},{32,6... | collective-permute-start | bytes 294920 | tf_op jit(solution)/shard_map/ppermute | solution.py:34
  13.8 6.9 %collective-permute-start.3 = (bf16[192,256]{1,0:T(8,128)(2,1)S(1)}, bf16[192,256]{1,0:T(8,128)(2,1)S(1)}, u32[]{:S(2)}, u32[]{:S(2)}) collective-permute-start(bf16[192,256]{1,0:T(8,128)(2,1)S(1)} %slice.59), channel_id=1, source_target_pairs={{0,96},{8,104},{16,112},{24,120},{4,100},{12,108},{20,116},{28,124... | collective-permute-start | bytes 294920 | tf_op jit(solution)/shard_map/ppermute | solution.py:34
  16.5 5.6 %collective-permute-start.7 = (bf16[384,256]{1,0:T(8,128)(2,1)S(1)}, bf16[384,256]{1,0:T(8,128)(2,1)S(1)}, u32[]{:S(2)}, u32[]{:S(2)}) collective-permute-start(bf16[384,256]{1,0:T(8,128)(2,1)S(1)} %collective-permute-done.2), channel_id=1, source_target_pairs={{0,8},{8,0},{16,24},{24,16},{4,12},{12,4},{20,28},{28,20},{32,40},... | collective-permute-start | bytes 589832 | tf_op jit(solution)/shard_map/ppermute | solution.py:34
  19.4 5.6 %collective-permute-start.8 = (bf16[384,256]{1,0:T(8,128)(2,1)S(1)}, bf16[384,256]{1,0:T(8,128)(2,1)S(1)}, u32[]{:S(2)}, u32[]{:S(2)}) collective-permute-start(bf16[384,256]{1,0:T(8,128)(2,1)S(1)} %collective-permute-done.2), channel_id=1, source_target_pairs={{0,20},{8,28},{16,0},{24,8},{4,16},{12,24},{20,4},{28,12},{32,52},... | collective-permute-start | bytes 589832 | tf_op jit(solution)/shard_map/ppermute | solution.py:34
  20.7 18.8 %collective-permute-start.10 = (bf16[384,256]{1,0:T(8,128)(2,1)S(1)}, bf16[384,256]{1,0:T(8,128)(2,1)S(1)}, u32[]{:S(2)}, u32[]{:S(2)}) collective-permute-start(bf16[384,256]{1,0:T(8,128)(2,1)S(1)} %collective-permute-done), channel_id=1, source_target_pairs={{0,8},{8,0},{16,24},{24,16},{4,12},{12,4},{20,28},{28,20},{32,40},... | collective-permute-start | bytes 589832 | tf_op jit(solution)/shard_map/ppermute | solution.py:34
  21.8 7.8 %collective-permute-start.11 = (bf16[384,256]{1,0:T(8,128)(2,1)S(1)}, bf16[384,256]{1,0:T(8,128)(2,1)S(1)}, u32[]{:S(2)}, u32[]{:S(2)}) collective-permute-start(bf16[384,256]{1,0:T(8,128)(2,1)S(1)} %collective-permute-done), channel_id=1, source_target_pairs={{0,16},{8,24},{16,4},{24,12},{4,20},{12,28},{20,0},{28,8},{32,48},... | collective-permute-start | bytes 589832 | tf_op jit(solution)/shard_map/ppermute | solution.py:34
  22.1 8.4 %collective-permute-start.15 = (bf16[384,256]{1,0:T(8,128)(2,1)S(1)}, bf16[384,256]{1,0:T(8,128)(2,1)S(1)}, u32[]{:S(2)}, u32[]{:S(2)}) collective-permute-start(bf16[384,256]{1,0:T(8,128)(2,1)S(1)} %collective-permute-done.14), channel_id=1, source_target_pairs={{0,8},{8,0},{16,24},{24,16},{4,12},{12,4},{20,28},{28,20},{32,40},... | collective-permute-start | bytes 589832 | tf_op jit(solution)/shard_map/ppermute | solution.py:34
  25.0 14.4 %collective-permute-start.4 = (bf16[384,256]{1,0:T(8,128)(2,1)S(1)}, bf16[384,256]{1,0:T(8,128)(2,1)S(1)}, u32[]{:S(2)}, u32[]{:S(2)}) collective-permute-start(bf16[384,256]{1,0:T(8,128)(2,1)S(1)} %get-tuple-element.75), channel_id=1, source_target_pairs={{0,8},{8,0},{16,24},{24,16},{4,12},{12,4},{20,28},{28,20},{32,40},... | collective-permute-start | bytes 589832 | tf_op jit(solution)/shard_map/ppermute | solution.py:34
  26.7 11.9 %collective-permute-start.5 = (bf16[384,256]{1,0:T(8,128)(2,1)S(1)}, bf16[384,256]{1,0:T(8,128)(2,1)S(1)}, u32[]{:S(2)}, u32[]{:S(2)}) collective-permute-start(bf16[384,256]{1,0:T(8,128)(2,1)S(1)} %get-tuple-element.75), channel_id=1, source_target_pairs={{0,20},{8,28},{16,0},{24,8},{4,16},{12,24},{20,4},{28,12},{32,52},... | collective-permute-start | bytes 589832 | tf_op jit(solution)/shard_map/ppermute | solution.py:34
  29.6 9.8 %collective-permute-start.9 = (bf16[384,256]{1,0:T(8,128)(2,1)S(1)}, bf16[384,256]{1,0:T(8,128)(2,1)S(1)}, u32[]{:S(2)}, u32[]{:S(2)}) collective-permute-start(bf16[384,256]{1,0:T(8,128)(2,1)S(1)} %collective-permute-done.8), channel_id=1, source_target_pairs={{0,8},{8,0},{16,24},{24,16},{4,12},{12,4},{20,28},{28,20},{32,40},... | collective-permute-start | bytes 589832 | tf_op jit(solution)/shard_map/ppermute | solution.py:34
  30.4 9.1 %collective-permute-start.12 = (bf16[384,256]{1,0:T(8,128)(2,1)S(1)}, bf16[384,256]{1,0:T(8,128)(2,1)S(1)}, u32[]{:S(2)}, u32[]{:S(2)}) collective-permute-start(bf16[384,256]{1,0:T(8,128)(2,1)S(1)} %collective-permute-done.11), channel_id=1, source_target_pairs={{0,8},{8,0},{16,24},{24,16},{4,12},{12,4},{20,28},{28,20},{32,40},... | collective-permute-start | bytes 589832 | tf_op jit(solution)/shard_map/ppermute | solution.py:34
  38.6 13.7 %collective-permute-start.6 = (bf16[384,256]{1,0:T(8,128)(2,1)S(1)}, bf16[384,256]{1,0:T(8,128)(2,1)S(1)}, u32[]{:S(2)}, u32[]{:S(2)}) collective-permute-start(bf16[384,256]{1,0:T(8,128)(2,1)S(1)} %collective-permute-done.5), channel_id=1, source_target_pairs={{0,8},{8,0},{16,24},{24,16},{4,12},{12,4},{20,28},{28,20},{32,40},... | collective-permute-start | bytes 589832 | tf_op jit(solution)/shard_map/ppermute | solution.py:34
  39.6 1.2 copy-start.3
  52.3 0.9 copy-start.4
  71.8 19.1 %copy-start.5 = (bf16[768,256]{1,0:T(8,128)(2,1)S(1)}, bf16[768,256]{1,0:T(8,128)(2,1)}, u32[]{:S(2)}) copy-start(bf16[768,256]{1,0:T(8,128)(2,1)} %get-tuple-element.62) | copy-start | bytes 1179652
  90.8 15.7 %collective-permute-start.17 = (bf16[1536,256]{1,0:T(8,128)(2,1)}, bf16[1536,256]{1,0:T(8,128)(2,1)S(1)}, u32[]{:S(2)}, u32[]{:S(2)}) collective-permute-start(bf16[1536,256]{1,0:T(8,128)(2,1)} %get-tuple-element.60), channel_id=1, source_target_pairs={{0,8},{8,0},{16,24},{24,16},{4,12},{12,4},{20,28},{28,20},{32,40},... | collective-permute-start | bytes 2359304 | tf_op jit(solution)/shard_map/ppermute | solution.py:34
  90.9 12.7 %collective-permute-start.18 = (bf16[768,256]{1,0:T(8,128)(2,1)S(1)}, bf16[768,256]{1,0:T(8,128)(2,1)S(1)}, u32[]{:S(2)}, u32[]{:S(2)}) collective-permute-start(bf16[768,256]{1,0:T(8,128)(2,1)S(1)} %copy-done.5), channel_id=1, source_target_pairs={{0,8},{8,0},{16,24},{24,16},{4,12},{12,4},{20,28},{28,20},{32,40},... | collective-permute-start | bytes 1179656 | tf_op jit(solution)/shard_map/ppermute | solution.py:34
  91.4 12.2 %copy-start.1 = (f32[768,256]{1,0:T(8,128)S(1)}, f32[768,256]{1,0:T(8,128)}, u32[]{:S(2)}) copy-start(f32[768,256]{1,0:T(8,128)} %get-tuple-element.61) | copy-start | bytes 2359300
  103.2 3.3 %copy-start = (f32[1536,256]{1,0:T(8,128)S(1)}, f32[1536,256]{1,0:T(8,128)}, u32[]{:S(2)}) copy-start(f32[1536,256]{1,0:T(8,128)} %get-tuple-element.59) | copy-start | bytes 4718596
  103.2 10.9 %collective-permute-start.16 = (bf16[768,256]{1,0:T(8,128)(2,1)}, bf16[768,256]{1,0:T(8,128)(2,1)S(1)}, u32[]{:S(2)}, u32[]{:S(2)}) collective-permute-start(bf16[768,256]{1,0:T(8,128)(2,1)} %get-tuple-element.58), channel_id=1, source_target_pairs={{0,8},{8,0},{16,24},{24,16},{4,12},{12,4},{20,28},{28,20},{32,40},... | collective-permute-start | bytes 1179656 | tf_op jit(solution)/shard_map/ppermute | solution.py:34
  103.7 7.6 %collective-permute-start.19 = (bf16[768,128]{1,0:T(8,128)(2,1)S(1)}, bf16[768,128]{1,0:T(8,128)(2,1)S(1)}, u32[]{:S(2)}, u32[]{:S(2)}) collective-permute-start(bf16[768,128]{1,0:T(8,128)(2,1)S(1)} %get-tuple-element.69), channel_id=1, source_target_pairs={{0,32},{8,40},{16,48},{24,56},{4,36},{12,44},{20,52},{28,60},{32,6... | collective-permute-start | bytes 589832 | tf_op jit(solution)/shard_map/ppermute | solution.py:34
  103.8 7.5 %collective-permute-start.21 = (bf16[768,128]{1,0:T(8,128)(2,1)S(1)}, bf16[768,128]{1,0:T(8,128)(2,1)S(1)}, u32[]{:S(2)}, u32[]{:S(2)}) collective-permute-start(bf16[768,128]{1,0:T(8,128)(2,1)S(1)} %get-tuple-element.70), channel_id=1, source_target_pairs={{0,96},{8,104},{16,112},{24,120},{4,100},{12,108},{20,116},{28,124... | collective-permute-start | bytes 589832 | tf_op jit(solution)/shard_map/ppermute | solution.py:34
  111.4 12.9 %copy-start.2 = (f32[768,256]{1,0:T(8,128)S(1)}, f32[768,256]{1,0:T(8,128)}, u32[]{:S(2)}) copy-start(f32[768,256]{1,0:T(8,128)} %get-tuple-element.57) | copy-start | bytes 2359300
  111.5 9.7 %collective-permute-start.22 = (bf16[768,256]{1,0:T(8,128)(2,1)S(1)}, bf16[768,256]{1,0:T(8,128)(2,1)S(1)}, u32[]{:S(2)}, u32[]{:S(2)}) collective-permute-start(bf16[768,256]{1,0:T(8,128)(2,1)S(1)} %pad_maximum_fusion.2), channel_id=1, source_target_pairs={{0,96},{8,104},{16,112},{24,120},{4,100},{12,108},{20,116},{28,124... | collective-permute-start | bytes 1179656 | tf_op jit(solution)/shard_map/ppermute | solution.py:34
  114.0 10.3 %collective-permute-start.20 = (bf16[768,256]{1,0:T(8,128)(2,1)S(1)}, bf16[768,256]{1,0:T(8,128)(2,1)S(1)}, u32[]{:S(2)}, u32[]{:S(2)}) collective-permute-start(bf16[768,256]{1,0:T(8,128)(2,1)S(1)} %pad_maximum_fusion.1), channel_id=1, source_target_pairs={{0,32},{8,40},{16,48},{24,56},{4,36},{12,44},{20,52},{28,60},{32,6... | collective-permute-start | bytes 1179656 | tf_op jit(solution)/shard_map/ppermute | solution.py:34
  124.5 7.1 %collective-permute-start.25 = (bf16[192,256]{1,0:T(8,128)(2,1)S(1)}, bf16[192,256]{1,0:T(8,128)(2,1)S(1)}, u32[]{:S(2)}, u32[]{:S(2)}) collective-permute-start(bf16[192,256]{1,0:T(8,128)(2,1)S(1)} %get-tuple-element.72), channel_id=1, source_target_pairs={{0,20},{8,28},{16,0},{24,8},{4,16},{12,24},{20,4},{28,12},{32,52},... | collective-permute-start | bytes 294920 | tf_op jit(solution)/shard_map/ppermute | solution.py:34
  125.0 6.6 %collective-permute-start.24 = (bf16[192,256]{1,0:T(8,128)(2,1)S(1)}, bf16[192,256]{1,0:T(8,128)(2,1)S(1)}, u32[]{:S(2)}, u32[]{:S(2)}) collective-permute-start(bf16[192,256]{1,0:T(8,128)(2,1)S(1)} %get-tuple-element.71), channel_id=1, source_target_pairs={{0,16},{8,24},{16,4},{24,12},{4,20},{12,28},{20,0},{28,8},{32,48},... | collective-permute-start | bytes 294920 | tf_op jit(solution)/shard_map/ppermute | solution.py:34
  126.1 5.5 %collective-permute-start.23 = (bf16[192,256]{1,0:T(8,128)(2,1)S(1)}, bf16[192,256]{1,0:T(8,128)(2,1)S(1)}, u32[]{:S(2)}, u32[]{:S(2)}) collective-permute-start(bf16[192,256]{1,0:T(8,128)(2,1)S(1)} %fusion.5), channel_id=1, source_target_pairs={{0,4},{8,12},{16,20},{24,28},{4,0},{12,8},{20,16},{28,24},{32,36},... | collective-permute-start | bytes 294920 | tf_op jit(solution)/shard_map/ppermute | solution.py:34
